TPU v7x, 32 devices: a whole 2x2x4 slice. The times are simulated.
32 devices in a mesh: rows: 8 (over z, x), blk: 4 (over y, core).
Axes of the slice: x: 2, y: 2, z: 4, core: 2. Of those that a mesh axis runs over, the one named last changes fastest.
Arguments:
- block_weight: bfloat16 [8, 4, 4, 64, 128, 128], P('rows', 'blk'), may hold values from 0.049804688 to 50
- block_row: int32 [8, 4, 4, 64], P('rows', 'blk'), may hold values from 0 to 15, as said below
- block_col: int32 [8, 4, 4, 64], P('rows', 'blk'), may hold values from 0 to 7, as said below
- block_count: int32 [8, 4, 4], P('rows', 'blk'), may hold values from 1 to 64, as said below
- block_samples: int32 [8, 4, 4, 64], P('rows', 'blk'), may hold values from 1 to 8
- row_degree: float32 [8, 4, 2048], P('rows', 'blk'), may hold values from 0.125 to 8
- col_degree: float32 [4, 1024], P('blk', 'rows'), may hold values from 1 to 8
- test_matrix: bfloat16 [4, 1024, 128], P('blk', 'rows'), may hold values from -6 to 6
Outputs:
- basis: float32 [8, 4, 2048, 128], P('rows', 'blk')
- triangle: float32 [128, 128], replicated
Inputs may be any that keep to these rules, and one draw needn't show every extreme that they name: Within one band and slab, the slots k < 64 hold distinct (block_row, block_col) pairs. `block_col`: see block_row: pairs are distinct within one band and slab. `block_count`: some band and slab has all 64 slots live in every draw.
All inputs are finite; a program needn't handle non-finite values.
Results may differ from a plain program's by a relative error of at most 0.0065.
Values may be sent and summed in bfloat16 or wider, within the bound.
No kernel may reach another device: no remote copies, remote signals or barrier semaphores. Data moves between devices by JAX's collectives and lax.ppermute only.
A program may use at most 64 MiB of HBM per device.

v0:
```python
import jax
import jax.numpy as jnp
from jax import lax
from jax.sharding import PartitionSpec as P

scale_factor = 16.0


def tile_update(
    running, weights, rows_idx, cols_idx, live_count, samples, row_deg, slab_rows, slab_deg
):
    block_edge = weights.shape[-1]
    capacity = weights.shape[0]
    band_blocks = running.shape[0]
    slab_blocks = slab_rows.shape[0] // block_edge
    slab_tiles = slab_rows.reshape(slab_blocks, block_edge, slab_rows.shape[1])
    picked = slab_tiles[cols_idx]
    col_d = slab_deg.reshape(slab_blocks, block_edge)[cols_idx]
    row_d = row_deg.reshape(band_blocks, block_edge)[rows_idx]
    scaled_ratio = (
        scale_factor
        * weights.astype(jnp.float32)
        / (samples.astype(jnp.float32)[:, None, None] * row_d[:, :, None] * col_d[:, None, :])
    )
    entries = jnp.log(jnp.maximum(scaled_ratio, 1.0)).astype(jnp.bfloat16)
    products = jnp.einsum("kij,kjc->kic", entries, picked, preferred_element_type=jnp.float32)
    alive_mask = (jnp.arange(capacity, dtype=jnp.int32) < live_count).astype(jnp.float32)
    chooser = (rows_idx[None, :] == jnp.arange(band_blocks, dtype=jnp.int32)[:, None]).astype(
        jnp.float32
    ) * alive_mask[None, :]
    return running + jnp.einsum("rk,kic->ric", chooser, products, precision=lax.Precision.HIGHEST)


def body(
    block_weight,
    block_row,
    block_col,
    block_count,
    block_samples,
    row_degree,
    col_degree,
    test_matrix,
):
    loop_size = lax.axis_size("blk")
    weights_all = block_weight[0, 0]
    rows_all = block_row[0, 0]
    cols_all = block_col[0, 0]
    counts_all = block_count[0, 0]
    samples_all = block_samples[0, 0]
    row_deg = row_degree[0, 0]
    block_edge = weights_all.shape[-1]
    band_blocks = row_deg.shape[0] // block_edge
    running = jnp.zeros((band_blocks, block_edge, test_matrix.shape[2]), jnp.float32)
    band_count = lax.axis_size("rows")
    piece_len = test_matrix.shape[1]
    sketch_width = test_matrix.shape[2]
    every_rows, every_deg = (
        lax.all_gather(test_matrix, ("rows", "blk"), axis=0, tiled=True),
        lax.all_gather(col_degree.astype(jnp.bfloat16), ("rows", "blk"), axis=0, tiled=True).astype(
            col_degree.dtype
        ),
    )
    whole_rows = (
        every_rows.reshape(band_count, loop_size, piece_len, sketch_width)
        .transpose(1, 0, 2, 3)
        .reshape(loop_size, band_count * piece_len, sketch_width)
    )
    whole_deg = (
        every_deg.reshape(band_count, loop_size, piece_len)
        .transpose(1, 0, 2)
        .reshape(loop_size, band_count * piece_len)
    )
    for s in range(loop_size):
        slab_index = s
        slab_index = jnp.asarray(slab_index).astype(jnp.int32)
        running = tile_update(
            running,
            lax.dynamic_index_in_dim(weights_all, slab_index, 0, keepdims=False),
            lax.dynamic_index_in_dim(rows_all, slab_index, 0, keepdims=False),
            lax.dynamic_index_in_dim(cols_all, slab_index, 0, keepdims=False),
            lax.dynamic_index_in_dim(counts_all, slab_index, 0, keepdims=False),
            lax.dynamic_index_in_dim(samples_all, slab_index, 0, keepdims=False),
            row_deg,
            whole_rows[s],
            whole_deg[s],
        )
    flat_rows = running.reshape(band_blocks * block_edge, running.shape[2])
    gram_local = jnp.dot(
        flat_rows.T, flat_rows, precision=lax.Precision.HIGHEST, preferred_element_type=jnp.float32
    )
    gram_total = lax.psum(gram_local, ("rows", "blk"))
    lower_factor = jnp.linalg.cholesky(gram_total)
    total_rows = flat_rows.shape[0] * lax.axis_size("rows") * loop_size
    root = jnp.sqrt(jnp.float32(total_rows))
    basis_rows = (
        lax.linalg.triangular_solve(
            lower_factor, flat_rows, left_side=False, lower=True, transpose_a=True
        )
        * root
    )
    return (basis_rows.reshape(1, 1, flat_rows.shape[0], flat_rows.shape[1]), lower_factor.T / root)


def solution(mesh):
    placed = (
        P("rows", "blk", None, None, None, None),
        P("rows", "blk", None, None),
        P("rows", "blk", None, None),
        P("rows", "blk", None),
        P("rows", "blk", None, None),
        P("rows", "blk", None),
        P("blk", "rows"),
        P("blk", "rows", None),
    )
    return jax.shard_map(
        body,
        mesh=mesh,
        in_specs=placed,
        out_specs=(P("rows", "blk", None, None), P()),
        check_vma=False,
    )
```

profile of v0, /device:TPU:0, one launch (start us, length us, event | category | flops | bytes accessed | tf_op | source)
XLA Modules:
  0.0 259.8 jit_solution(12312104870430039245)
XLA Ops:
  7.2 0.7 all-gather.3.cloned.1.call-update
  8.0 0.8 fusion.86
  8.8 0.8 fusion.87
  9.6 0.7 convert_bitcast_fusion.3
  10.3 43.0 %all-gather = bf16[32,1,128]{2,1,0:T(2,128)(2,1)S(1)} all-gather(bf16[1,1,128]{2,1,0:T(2,128)(2,1)S(1)} %convert_bitcast_fusion.3), channel_id=1, replica_groups=mesh['rows'=8,'blk'=4] {'rows','blk'}, dimensions={0}, use_global_device_ids=true | all-gather | bytes 8448 | tf_op jit(solution)/shard_map/all_gather | solution.py:59
  53.4 0.6 gather_fusion.3
  54.0 0.6 gather_fusion
  54.6 0.6 gather_fusion.6
  55.2 0.6 gather_fusion.9
  55.7 0.6 gather_fusion.4
  56.3 0.6 gather_fusion.1
  57.0 0.6 gather_fusion.7
  57.6 0.6 gather_fusion.10
  58.1 1.5 fusion.100
  59.6 0.6 compare_convert_fusion.2
  60.3 0.6 compare_convert_fusion.3
  60.9 0.7 compare_convert_fusion.1
  61.6 0.7 compare_convert_fusion
  62.2 0.8 slice_bitcast_fusion.8
  63.1 0.8 convert_bitcast_fusion
  63.9 0.1 broadcast_multiply_fusion.2
  64.1 0.1 broadcast_multiply_fusion.1
  64.1 0.1 broadcast_multiply_fusion
  64.2 3.2 %all-gather.3.cloned.1.call-done = bf16[32,128,128]{2,1,0:T(8,128)(2,1)} async-done(((bf16[1,128,128]{2,1,0:T(8,128)(2,1)}), bf16[32,128,128]{2,1,0:T(8,128)(2,1)}) %all-gather.3.cloned.1.call-update) | async-done | bytes 1048592 | tf_op jit(solution)/shard_map/all_gather | solution.py:58
  67.4 1.3 slice_bitcast_fusion
  68.7 2.1 gather_fusion.5
  70.9 2.1 gather_fusion.2
  73.0 0.9 gather_fusion.8
  74.0 2.2 gather_fusion.11
  76.1 3.1 %fusion.23 = f32[64,128,128]{2,1,0:T(8,128)S(1)} fusion(bf16[64,128,128]{2,1,0:T(8,128)(2,1)} %gather_fusion.5, f32[64,128]{1,0:T(8,128)S(1)} %gather_fusion.4, f32[64,128]{1,0:T(8,128)S(1)} %broadcast_multiply_fusion.2, bf16[1,1,4,64,128,128]{5,4,3,2,1,0:T(8,128)(2,1)} %param.8), kind=kOutput, calls=%fused_computation.39 | convolution fusion | flops 274726912 | bytes 8454144 | tf_op jit(solution)/shard_map/kij,kjc->kic/dot_general | solution.py:26
  79.3 4.4 %fusion.16 = f32[16,128,128]{2,0,1:T(8,128)S(1)} fusion(f32[64,128,128]{2,1,0:T(8,128)S(1)} %fusion.23, f32[64]{0:T(128)S(1)} %compare_convert_fusion.2, s32[64]{0:T(128)S(1)} %get-tuple-element.19), kind=kOutput, calls=%fused_computation.32 | convolution fusion | flops 201328640 | bytes 5243392 | tf_op jit(solution)/shard_map/rk,kic->ric/dot_general | solution.py:31
  83.7 3.8 %fusion.21 = f32[64,128,128]{2,1,0:T(8,128)S(1)} fusion(bf16[64,128,128]{2,1,0:T(8,128)(2,1)S(1)} %copy-done.2, f32[64,128]{1,0:T(8,128)S(1)} %gather_fusion.1, f32[64,128]{1,0:T(8,128)S(1)} %broadcast_multiply_fusion.3, bf16[1,1,4,64,128,128]{5,4,3,2,1,0:T(8,128)(2,1)} %param.8), kind=kOutput, calls=%fused_computation.38 | convolution fusion | flops 274726912 | bytes 8454144 | tf_op jit(solution)/shard_map/kij,kjc->kic/dot_general | solution.py:26
  87.5 2.8 %fusion.25 = f32[64,128,128]{2,1,0:T(8,128)S(1)} fusion(bf16[64,128,128]{2,1,0:T(8,128)(2,1)S(1)} %gather_fusion.8, f32[64,128]{1,0:T(8,128)S(1)} %gather_fusion.7, f32[64,128]{1,0:T(8,128)S(1)} %broadcast_multiply_fusion.1, bf16[1,1,4,64,128,128]{5,4,3,2,1,0:T(8,128)(2,1)S(1)} %bitcast.159), kind=kOutput, calls=%fused_computation.40 | convolution fusion | flops 274726912 | bytes 8454144 | tf_op jit(solution)/shard_map/kij,kjc->kic/dot_general | solution.py:26
  90.2 2.9 %fusion.27 = f32[64,128,128]{2,1,0:T(8,128)S(1)} fusion(bf16[64,128,128]{2,1,0:T(8,128)(2,1)S(1)} %copy-done.1, f32[64,128]{1,0:T(8,128)S(1)} %gather_fusion.10, f32[64,128]{1,0:T(8,128)S(1)} %broadcast_multiply_fusion, bf16[1,1,4,64,128,128]{5,4,3,2,1,0:T(8,128)(2,1)S(1)} %bitcast.159), kind=kOutput, calls=%fused_computation.41 | convolution fusion | flops 274726912 | bytes 8454144 | tf_op jit(solution)/shard_map/kij,kjc->kic/dot_general | solution.py:26
  93.2 4.4 %fusion.49 = f32[16,128,128]{2,0,1:T(8,128)S(1)} fusion(f32[16,128,128]{2,0,1:T(8,128)S(1)} %fusion.16, f32[64,128,128]{2,1,0:T(8,128)S(1)} %fusion.21, f32[64]{0:T(128)S(1)} %compare_convert_fusion.3, s32[64]{0:T(128)S(1)} %get-tuple-element.20), kind=kOutput, calls=%fused_computation.62 | convolution fusion | flops 201590784 | bytes 6291968 | tf_op jit(solution)/shard_map/rk,kic->ric/dot_general | solution.py:31
  97.5 4.4 %fusion.52 = f32[16,128,128]{2,0,1:T(8,128)S(1)} fusion(f32[16,128,128]{2,0,1:T(8,128)S(1)} %fusion.49, f32[64,128,128]{2,1,0:T(8,128)S(1)} %fusion.25, f32[64]{0:T(128)S(1)} %compare_convert_fusion.1, s32[64]{0:T(128)S(1)} %get-tuple-element.21), kind=kOutput, calls=%fused_computation.63 | convolution fusion | flops 201590784 | bytes 6291968 | tf_op jit(solution)/shard_map/rk,kic->ric/dot_general | solution.py:31
  101.9 4.6 %fusion.55 = f32[16,128,128]{2,0,1:T(8,128)S(1)} fusion(f32[16,128,128]{2,0,1:T(8,128)S(1)} %fusion.52, f32[64,128,128]{2,1,0:T(8,128)S(1)} %fusion.27, f32[64]{0:T(128)S(1)} %compare_convert_fusion, s32[64]{0:T(128)S(1)} %get-tuple-element.18), kind=kOutput, calls=%fused_computation.64 | convolution fusion | flops 201590784 | bytes 6291968 | tf_op jit(solution)/shard_map/rk,kic->ric/dot_general | solution.py:31
  106.5 2.5 convolution_bitcast_fusion
  109.0 0.3 copy.28
  109.4 116.2 %all-reduce.2.cloned.1.call-done = f32[128,128]{0,1:T(8,128)} async-done(((f32[128,128]{0,1:T(8,128)}), f32[128,128]{0,1:T(8,128)}) %all-reduce.2.cloned.1.call-update) | async-done | bytes 65552 | tf_op jit(solution)/shard_map/psum | solution.py:91
  225.6 0.9 copy.30
  226.6 0.9 fusion.59
  227.4 11.7 %cholesky.16 = f32[128,128]{1,0:T(8,128)S(1)} custom-call(f32[128,128]{1,0:T(8,128)S(1)} %fusion.59), custom_call_target="Cholesky" | custom-call | tf_op jit(solution)/shard_map/jit(cholesky)/cholesky | solution.py:92
  239.2 0.6 compare_reduce_fusion
  239.8 0.7 multiply_bitcast_fusion
  240.5 9.8 %custom-call.6 = f32[1,128,128]{1,2,0:T(8,128)S(1)} custom-call(f32[1,128,128]{2,1,0:T(8,128)S(1)} %get-tuple-element.13), custom_call_target="InvertDiagBlocksLowerTriangular" | custom-call | tf_op jit(solution)/shard_map/triangular_solve | solution.py:96
  250.3 0.7 copy.31
  251.0 1.9 fusion.20
  (23 shorter events, 0.3 us)
Async XLA Ops:
  7.2 46.2 %copy-start = (f32[1,1,2048]{2,1,0:T(1,128)S(1)}, f32[1,1,2048]{2,1,0:T(1,128)}, u32[]{:S(2)}) copy-start(f32[1,1,2048]{2,1,0:T(1,128)} %param.13) | copy-start | bytes 24580
  7.2 60.2 %all-gather.3.cloned.1.call-start = ((), (), s32[]{:S(2)}) async-start(), calls=%async_computation | async-start | bytes 1081344 | tf_op jit(solution)/shard_map/all_gather | solution.py:58
  7.9 217.7 %all-reduce.2.cloned.1.call-start = ((), (), s32[]{:S(2)}) async-start(), calls=%async_computation.1 | async-start | bytes 131072 | tf_op jit(solution)/shard_map/psum | solution.py:91
  79.3 4.4 %copy-start.2 = (bf16[64,128,128]{2,1,0:T(8,128)(2,1)S(1)}, bf16[64,128,128]{2,1,0:T(8,128)(2,1)}, u32[]{:S(2)}) copy-start(bf16[64,128,128]{2,1,0:T(8,128)(2,1)} %gather_fusion.2) | copy-start | bytes 6291460
  79.3 8.2 %slice-start = ((s8[8388608]{0:T(1024)(128)(4,1)}), s8[4194304]{0:T(1024)(128)(4,1)S(1)}, s32[]{:S(2)}) async-start(s8[8388608]{0:T(1024)(128)(4,1)} %bitcast.158), calls=%async_computation.2 | async-start | bytes 8388608
  83.7 3.8 %slice-start.1 = ((s8[8388608]{0:T(1024)(128)(4,1)}), s8[4194304]{0:T(1024)(128)(4,1)S(1)}, s32[]{:S(2)}) async-start(s8[8388608]{0:T(1024)(128)(4,1)} %bitcast.158), calls=%async_computation.3 | async-start | bytes 8388608
  87.5 2.8 %copy-start.1 = (bf16[64,128,128]{2,1,0:T(8,128)(2,1)S(1)}, bf16[64,128,128]{2,1,0:T(8,128)(2,1)}, u32[]{:S(2)}) copy-start(bf16[64,128,128]{2,1,0:T(8,128)(2,1)} %gather_fusion.11) | copy-start | bytes 6291460
Sparse Core Ops, SparseCore 0:
  10.9 56.4 all-gather.2
  109.2 116.4 all-reduce.1
where the time goes:
time: 261 us; the launch traced here: 260 us
  waiting for transfers between devices  120 us (46%)
  blocking collectives  43 us (16%)
  matrix products  34.7 us (13%)
  other arithmetic  29.8 us (11%)
  local copies, waits for them, and re-layouts  17.8 us (7%)
  between operations  14.3 us (5%)
    psum x1, waiting for transfers between devices, body(): gram_total = lax.psum(gram_local, ('rows', 'blk'))  116 us
    all_gather x1, blocking collectives, body(): lax.all_gather(col_degree.astype(jnp.bfloat16), ('rows', 'blk'), axis=0,...  43 us
    dot_general x4, matrix products, tile_update(): jnp.einsum('rk,kic->ric', chooser, products, precision=lax.Precision.HIGH...  17.7 us
    dot_general x4, matrix products, tile_update(): jnp.einsum('kij,kjc->kic', entries, picked, preferred_element_type=jnp.fl...  12.6 us
    another operation x3, other arithmetic, body(): lower_factor = jnp.linalg.cholesky(gram_total)  12.4 us
    another operation x1, other arithmetic, body(): lax.linalg.triangular_solve(lower_factor, flat_rows, left_side=False, low...  9.81 us
    gather x4, local copies, waits for them, and re-layouts, tile_update(): picked = slab_tiles[cols_idx]  7.41 us
  transfers between devices with their start and end apart: 2, of which 2 were waited for; matrix products, arithmetic and copies ran while one was open for 5% of the time, Pallas kernels for 0%

commit v1 on v0

v1 whole, which is shorter than its diff:
```python
import functools
import math

import jax
import jax.numpy as jnp
from jax import lax
from jax.experimental import pallas as pl
from jax.experimental.pallas import tpu as pltpu
from jax.sharding import PartitionSpec as P

SCALE = 16.0
GROUP = 4
CHUNK = 8


def sketch_kernel(tile, w_hbm, row_s, col_s, cnt_s, samp_s, tab_s, rd_ref, g_ref,
                  hi_ref, lo_ref, gram_ref, wbuf, x_ref, rb_ref, lc_ref, acc_ref, sem,
                  off_s, cur_s, ct_s):
    slabs, cap = w_hbm.shape[0], w_hbm.shape[1]
    bands = rd_ref.shape[0]
    n = tile
    trash = x_ref.shape[0] - 1
    zero = trash - 1
    chunks = cap // CHUNK

    def copy(s, c):
        return pltpu.make_async_copy(w_hbm.at[s, pl.ds(c * CHUNK, CHUNK)], wbuf.at[s, pl.ds(c * CHUNK, CHUNK)],
                                     sem.at[s, c])

    for s in range(slabs):
        for c in range(chunks):
            @pl.when(c * CHUNK < cnt_s[s])
            def _():
                copy(s, c).start()

    for q in range(bands):
        rb_ref[q] = jnp.transpose(jnp.broadcast_to(1.0 / rd_ref[q:q + 1, :], (n, n)))
    def deg(l, carry):
        d = g_ref[l, n:n + 16, :].astype(jnp.float32)
        lc_ref[l] = jnp.broadcast_to(jnp.log(d[0:1] + d[1:2] + d[2:3]), (8, n))
        return carry
    lax.fori_loop(0, g_ref.shape[0], deg, 0)

    for q in range(bands):
        cur_s[q] = 0
    for s in range(slabs):
        def count(k, carry):
            q = row_s[s, k]
            cur_s[q] = cur_s[q] + 1
            return carry
        lax.fori_loop(0, cnt_s[s], count, 0)
    total = jnp.int32(0)
    most = jnp.int32(0)
    for q in range(bands):
        c = cur_s[q]
        off_s[q] = total
        off_s[bands + q] = total + c
        cur_s[q] = total
        total = total + ((c + 1) // 2) * 2
        most = jnp.maximum(most, c)
    x_ref[zero] = jnp.full((n, n), -1e30, jnp.float32)
    ct_s[zero] = 0

    for s in range(slabs):
        live = cnt_s[s]
        def chunk(c, carry):
            copy(s, c).wait()
            for g0 in range(0, CHUNK, GROUP):
                todo = []
                for j in range(GROUP):
                    k = c * CHUNK + g0 + j
                    ok = k < live
                    q = row_s[s, k]
                    p = cur_s[q]
                    cur_s[q] = p + ok.astype(jnp.int32)
                    dest = jnp.where(ok, p, trash)
                    ct_s[dest] = tab_s[col_s[s, k] * slabs + s]
                    todo.append((k, q, dest, SCALE / samp_s[s, k].astype(jnp.float32)))
                out = []
                for k, q, dest, sc in todo:
                    out.append(jnp.log(wbuf[s, k].astype(jnp.float32) * (rb_ref[q] * sc)))
                for (k, q, dest, sc), o in zip(todo, out):
                    x_ref[dest] = o
            return carry
        lax.fori_loop(0, (live + CHUNK - 1) // CHUNK, chunk, 0)

    acc_ref[...] = jnp.zeros_like(acc_ref)

    def step(it, carry):
        for q in range(bands):
            e, t = [], []
            for j in range(2):
                i = off_s[q] + 2 * it + j
                i = jnp.where(i < off_s[bands + q], i, zero)
                l = ct_s[i]
                y = x_ref[i].reshape(n // 8, 8, n) - lc_ref[l][None]
                e.append(jnp.maximum(y, 0.0).reshape(n, n).astype(jnp.bfloat16))
                t.append(g_ref[l, 0:n, :])
            acc_ref[q] += jnp.dot(jnp.concatenate(e, axis=1), jnp.concatenate(t, axis=0),
                                  preferred_element_type=jnp.float32)
        return carry
    lax.fori_loop(0, (most + 1) // 2, step, 0)

    gram = jnp.zeros((n, 2 * n), jnp.float32)
    for q in range(bands):
        a = acc_ref[q]
        h = a.astype(jnp.bfloat16)
        l = (a - h.astype(jnp.float32)).astype(jnp.bfloat16)
        hi_ref[q * n:(q + 1) * n, :] = h
        lo_ref[q * n:(q + 1) * n, :] = l
        gram = gram + lax.dot_general(h, jnp.concatenate([h, l], axis=1), (((0,), (0,)), ((), ())),
                                      preferred_element_type=jnp.float32)
    cross = gram[:, n:]
    gram_ref[...] = gram[:, :n] + (cross + jnp.transpose(cross))


def sketch(w, rows, cols, counts, samples, tab, rd, g):
    slabs, cap, n, _ = w.shape
    bands = rd.shape[0]
    S = pl.BlockSpec(memory_space=pltpu.SMEM)
    V = pl.BlockSpec(memory_space=pltpu.VMEM)
    blocks = slabs * cap + 2 * bands + 2
    return pl.pallas_call(
        functools.partial(sketch_kernel, n),
        out_shape=(jax.ShapeDtypeStruct((bands * n, n), jnp.bfloat16), jax.ShapeDtypeStruct((bands * n, n), jnp.bfloat16),
                   jax.ShapeDtypeStruct((n, n), jnp.float32)),
        in_specs=[pl.BlockSpec(memory_space=pl.ANY), S, S, S, S, S, V, V],
        out_specs=(V, V, V),
        scratch_shapes=[
            pltpu.VMEM((slabs, cap, n, n), jnp.bfloat16),
            pltpu.VMEM((blocks, n, n), jnp.float32),
            pltpu.VMEM((bands, n, n), jnp.float32),
            pltpu.VMEM((g.shape[0], 8, n), jnp.float32),
            pltpu.VMEM((bands, n, n), jnp.float32),
            pltpu.SemaphoreType.DMA((slabs, cap // CHUNK)),
            pltpu.SMEM((2 * bands,), jnp.int32),
            pltpu.SMEM((bands,), jnp.int32),
            pltpu.SMEM((blocks,), jnp.int32),
        ],
        compiler_params=pltpu.CompilerParams(vmem_limit_bytes=48 << 20),
        name="sketch_gram",
    )(w, rows, cols, counts, samples, tab, rd, g)

def _rep(x, n):
    return jnp.broadcast_to(x, (1, n))

def solve_kernel(nb, root, chunk, gram_ref, hi_ref, lo_ref, basis_ref, tri_ref, m_ref, u_ref):
    n = gram_ref.shape[0]
    ii = lax.broadcasted_iota(jnp.int32, (n, n), 0)
    jj = lax.broadcasted_iota(jnp.int32, (n, n), 1)
    m_ref[:, :n] = gram_ref[...]
    m_ref[:, n:] = (ii == jj).astype(jnp.float32)
    for r0 in range(0, n, nb):
        panel = m_ref[r0:r0 + nb, :]
        left = [panel[t:t + 1, :n] for t in range(nb)]
        right = [panel[t:t + 1, n:] for t in range(nb)]
        s = [[_rep(panel[t:t + 1, r0 + u:r0 + u + 1], n) if u >= t else None for u in range(nb)] for t in range(nb)]
        for t in range(nb):
            r = lax.rsqrt(s[t][t])
            left[t] = left[t] * r
            right[t] = right[t] * r
            f = [s[t][u] * r if u > t else None for u in range(nb)]
            for u in range(t + 1, nb):
                left[u] = left[u] - f[u] * left[t]
                right[u] = right[u] - f[u] * right[t]
                for v in range(u, nb):
                    s[u][v] = s[u][v] - f[u] * f[v]
        u_l = jnp.concatenate(left, axis=0)
        u_r = jnp.concatenate(right, axis=0)
        u_ref[r0:r0 + nb, :n] = u_l
        u_ref[r0:r0 + nb, n:] = u_r
        if r0 + nb < n:
            full = jnp.concatenate([u_l, u_r], axis=1)
            upd = lax.dot_general(u_l, full, (((0,), (0,)), ((), ())), precision=lax.Precision.HIGHEST,
                                  preferred_element_type=jnp.float32)
            m_ref[r0 + nb:, :] = m_ref[r0 + nb:, :] - upd[r0 + nb:, :]
    tri_ref[...] = jnp.where(jj >= ii, u_ref[:, :n], 0.0) * (1.0 / root)
    w = jnp.where(jj <= ii, u_ref[:, n:], 0.0) * root
    wh = w.astype(jnp.bfloat16)
    wl = (w - wh.astype(jnp.float32)).astype(jnp.bfloat16)
    both = jnp.concatenate([wh, wl], axis=0)
    dims = (((1,), (1,)), ((), ()))
    for c in range(0, hi_ref.shape[0], chunk):
        h = hi_ref[c:c + chunk, :]
        l = lo_ref[c:c + chunk, :]
        a = lax.dot_general(h, both, dims, preferred_element_type=jnp.float32)
        b = lax.dot_general(l, wh, dims, preferred_element_type=jnp.float32)
        basis_ref[c:c + chunk, :] = a[:, :n] + (a[:, n:] + b)

def solve(gram, hi, lo, root, nb=16, chunk=256):
    n = gram.shape[0]
    V = pl.BlockSpec(memory_space=pltpu.VMEM)
    return pl.pallas_call(
        functools.partial(solve_kernel, nb, root, chunk),
        out_shape=(jax.ShapeDtypeStruct(hi.shape, jnp.float32), jax.ShapeDtypeStruct((n, n), jnp.float32)),
        in_specs=[V, V, V], out_specs=(V, V),
        scratch_shapes=[pltpu.VMEM((n, 2 * n), jnp.float32), pltpu.VMEM((n, 2 * n), jnp.float32)],
        compiler_params=pltpu.CompilerParams(vmem_limit_bytes=32 << 20),
        name="cholesky_basis",
    )(gram, hi, lo)


AXES = ("rows", "blk")
PAD = 16


def split3(x):
    parts = []
    for _ in range(3):
        h = lax.reduce_precision(x, 8, 7)
        parts.append(h.astype(jnp.bfloat16))
        x = x - h
    return parts


def gather_pieces(piece, n_dev):
    masks = [0]
    got = piece[None]
    bit = n_dev // 2
    while bit:
        other = lax.ppermute(got, AXES, [(i, i ^ bit) for i in range(n_dev)])
        got = jnp.concatenate([got, other], axis=0)
        masks = masks + [m ^ bit for m in masks]
        bit //= 2
    return got, masks


def sum_all(x, n_dev):
    n = x.shape[0]
    width = min(x.shape[1], x.size // n_dev)
    shares = x.reshape(n_dev, -1, width)
    mine = lax.all_to_all(shares, AXES, 0, 0, tiled=True).sum(axis=0)
    sent = jnp.broadcast_to(mine[None], shares.shape)
    return lax.all_to_all(sent, AXES, 0, 0, tiled=True).reshape(x.shape)


def body(block_weight, block_row, block_col, block_count, block_samples, row_degree, col_degree, test_matrix):
    n_rows, n_blk = lax.axis_size("rows"), lax.axis_size("blk")
    n_dev = n_rows * n_blk
    n = block_weight.shape[-1]
    piece_len, width = test_matrix.shape[1:]
    row_deg = row_degree[0, 0].reshape(-1, n)
    degs = jnp.stack(split3(col_degree[0]))
    piece = jnp.concatenate([test_matrix[0], jnp.pad(degs, ((0, PAD - 3), (0, width - piece_len)))], axis=0)
    pieces, masks = gather_pieces(piece, n_dev)
    me = lax.axis_index(AXES)
    table = me ^ jnp.asarray(masks, jnp.int32)
    if piece_len != n:
        share = n // piece_len
        ordered = pieces[jnp.argsort(table)]
        ordered = ordered.reshape(n_rows // share, share, n_blk, piece_len + PAD, width).transpose(0, 2, 1, 3, 4)
        ordered = ordered.reshape(-1, share, piece_len + PAD, width)
        tiles = ordered[:, :, :piece_len].reshape(-1, n, width)
        heads = ordered[:, :, piece_len:, :piece_len].transpose(0, 2, 1, 3).reshape(-1, PAD, n)
        pieces = jnp.concatenate([tiles, heads], axis=1)
        slots = jnp.arange(pieces.shape[0], dtype=jnp.int32)
    else:
        weights = [masks.index(1 << i) for i in range(n_dev.bit_length() - 1)]
        slots = jnp.zeros((n_dev,), jnp.int32)
        far = me ^ jnp.arange(n_dev, dtype=jnp.int32)
        for i, wt in enumerate(weights):
            slots = slots + ((far >> i) & 1) * wt
    hi, lo, gram = sketch(block_weight[0, 0], block_row[0, 0], block_col[0, 0], block_count[0, 0],
                          block_samples[0, 0], slots, row_deg, pieces)
    gram = sum_all(gram, n_dev)
    root = math.sqrt(hi.shape[0] * n_dev)
    basis, triangle = solve(gram, hi, lo, root)
    return basis[None, None], triangle


def solution(mesh):
    placed = (
        P("rows", "blk", None, None, None, None),
        P("rows", "blk", None, None),
        P("rows", "blk", None, None),
        P("rows", "blk", None),
        P("rows", "blk", None, None),
        P("rows", "blk", None),
        P("blk", "rows"),
        P("blk", "rows", None),
    )
    return jax.shard_map(
        body,
        mesh=mesh,
        in_specs=placed,
        out_specs=(P("rows", "blk", None, None), P()),
        check_vma=False,
    )
```

time: 261 us -> 70.4 us (0.27)
  waiting for transfers between devices: 120 us -> 14.6 us
  matrix products: 34.7 us -> 0 us
  other arithmetic: 29.8 us -> 2.32 us
  blocking collectives: 43 us -> 22.6 us
  Pallas kernels: 0 us -> 20.3 us
  local copies, waits for them, and re-layouts: 17.8 us -> 0.34 us
  between operations: 14.3 us -> 0.78 us
  starting transfers between devices: 0.08 us -> 9.25 us
    psum x1 -> x0, waiting for transfers between devices: 116 us -> none  [body(): gram_total = lax.psum(gram_local, ('rows', 'blk'))]
    all_gather x1 -> x0, blocking collectives: 43 us -> none  [body(): lax.all_gather(col_degree.astype(jnp.bfloat16), ('rows', 'blk'), axis=0,...]
    dot_general x9 -> x0, matrix products: 32.7 us -> none  [the longest x4 17.7 us: tile_update(): jnp.einsum('rk,kic->ric', chooser, products, precision=lax.Precision.HIGH...]
    all_to_all x0 -> x2, blocking collectives: none -> 22.6 us  [the longest x1 13.5 us: sum_all(): mine = lax.all_to_all(shares, AXES, 0, 0, tiled=True).sum(axis=0)]
    another operation x4 -> x1, other arithmetic: 22.2 us -> 0.01 us  [body(): degs = jnp.stack(split3(col_degree[0]))]
    pallas_call x0 -> x2, Pallas kernels: none -> 20.3 us  [the longest x1 12.5 us: sketch(): pl.pallas_call(functools.partial(sketch_kernel, n), out_shape=(jax.ShapeD...]
    ppermute x0 -> x5, waiting for transfers between devices: none -> 14.6 us  [gather_pieces(): other = lax.ppermute(got, AXES, [(i, i ^ bit) for i in range(n_dev)])]
    gather x12 -> x0, local copies, waits for them, and re-layouts: 12.2 us -> none  [the longest x4 7.41 us: tile_update(): picked = slab_tiles[cols_idx]]
  transfers between devices with their start and end apart: 2 -> 5, of which waited for: 2 -> 5; matrix products, arithmetic and copies ran while one was open for 5% -> 1% of each run, Pallas kernels for 0% -> 0%
where the time goes in v1:
time: 70.4 us; the launch traced here: 70.2 us
  blocking collectives  22.6 us (32%)
  Pallas kernels  20.3 us (29%)
  waiting for transfers between devices  14.6 us (21%)
  starting transfers between devices  9.25 us (13%)
  other arithmetic  2.32 us (3%)
  between operations  0.78 us (1%)
    ppermute x5, waiting for transfers between devices, gather_pieces(): other = lax.ppermute(got, AXES, [(i, i ^ bit) for i in range(n_dev)])  14.6 us
    all_to_all x1, blocking collectives, sum_all(): mine = lax.all_to_all(shares, AXES, 0, 0, tiled=True).sum(axis=0)  13.5 us
    pallas_call x1, Pallas kernels, sketch(): pl.pallas_call(functools.partial(sketch_kernel, n), out_shape=(jax.ShapeD...  12.5 us
    ppermute x5, starting transfers between devices, gather_pieces(): other = lax.ppermute(got, AXES, [(i, i ^ bit) for i in range(n_dev)])  9.25 us
    all_to_all x1, blocking collectives, sum_all(): return lax.all_to_all(sent, AXES, 0, 0, tiled=True).reshape(x.shape)  9.1 us
    pallas_call x1, Pallas kernels, solve(): pl.pallas_call(functools.partial(solve_kernel, nb, root, chunk), out_shap...  7.75 us
  transfers between devices with their start and end apart: 5, of which 5 were waited for; matrix products, arithmetic and copies ran while one was open for 1% of the time, Pallas kernels for 0%

profile of v1, /device:TPU:0, one launch (start us, length us, event | category | flops | bytes accessed | tf_op | source)
XLA Modules:
  0.0 70.2 jit_solution(14348451210183188786)
XLA Ops:
  0.6 0.7 reduce-precision_convert_fusion.1
  1.3 0.8 %maximum_bitcast_fusion = bf16[1,144,128]{2,1,0:T(8,128)(2,1)S(1)} fusion(bf16[16,128]{1,0:T(8,128)(2,1)S(1)} %fusion.4, bf16[128,128]{1,0:T(8,128)(2,1)} %bitcast.24), kind=kLoop, calls=%fused_computation.3 | loop fusion | flops 73728 | bytes 73728 | tf_op jit(solution)/shard_map/broadcast_in_dim | solution.py:218
  2.1 4.0 %collective-permute-start = (bf16[1,144,128]{2,1,0:T(8,128)(2,1)S(1)}, bf16[1,144,128]{2,1,0:T(8,128)(2,1)S(1)}, u32[]{:S(2)}, u32[]{:S(2)}) collective-permute-start(bf16[1,144,128]{2,1,0:T(8,128)(2,1)S(1)} %maximum_bitcast_fusion), channel_id=1, source_target_pairs={{0,16},{1,17},{2,18},{3,19},{4,20},{5,21},{6,22},{7,23},{8,24},{9,... | collective-permute-start | bytes 110600 | tf_op jit(solution)/shard_map/ppermute | solution.py:221
  6.1 2.3 %collective-permute-done = bf16[1,144,128]{2,1,0:T(8,128)(2,1)S(1)} collective-permute-done((bf16[1,144,128]{2,1,0:T(8,128)(2,1)S(1)}, bf16[1,144,128]{2,1,0:T(8,128)(2,1)S(1)}, u32[]{:S(2)}, u32[]{:S(2)}) %collective-permute-start) | collective-permute-done | bytes 36896 | tf_op jit(solution)/shard_map/ppermute | solution.py:221
  8.4 1.6 %collective-permute-start.1 = (bf16[2,144,128]{2,1,0:T(8,128)(2,1)S(1)}, bf16[2,144,128]{2,1,0:T(8,128)(2,1)S(1)}, u32[]{:S(2)}, u32[]{:S(2)}) collective-permute-start(bf16[2,144,128]{2,1,0:T(8,128)(2,1)S(1)} %pad_maximum_fusion.2), channel_id=1, source_target_pairs={{0,8},{1,9},{2,10},{3,11},{4,12},{5,13},{6,14},{7,15},{8,0},{9,1},... | collective-permute-start | bytes 221192 | tf_op jit(solution)/shard_map/ppermute | solution.py:221
  10.0 2.8 %collective-permute-done.1 = bf16[2,144,128]{2,1,0:T(8,128)(2,1)S(1)} collective-permute-done((bf16[2,144,128]{2,1,0:T(8,128)(2,1)S(1)}, bf16[2,144,128]{2,1,0:T(8,128)(2,1)S(1)}, u32[]{:S(2)}, u32[]{:S(2)}) %collective-permute-start.1) | collective-permute-done | bytes 73760 | tf_op jit(solution)/shard_map/ppermute | solution.py:221
  12.9 1.8 %collective-permute-start.2 = (bf16[4,144,128]{2,1,0:T(8,128)(2,1)S(1)}, bf16[4,144,128]{2,1,0:T(8,128)(2,1)S(1)}, u32[]{:S(2)}, u32[]{:S(2)}) collective-permute-start(bf16[4,144,128]{2,1,0:T(8,128)(2,1)S(1)} %pad_maximum_fusion.1), channel_id=1, source_target_pairs={{0,4},{1,5},{2,6},{3,7},{4,0},{5,1},{6,2},{7,3},{8,12},{9,13},{10,... | collective-permute-start | bytes 442376 | tf_op jit(solution)/shard_map/ppermute | solution.py:221
  14.7 0.8 %constant_dynamic-update-slice_fusion.4 = (bf16[16,144,128]{2,1,0:T(8,128)(2,1)S(1)}, bf16[32,144,128]{2,1,0:T(8,128)(2,1)S(1)}) fusion(bf16[16,128]{1,0:T(8,128)(2,1)S(1)} %fusion.4, bf16[128,128]{1,0:T(8,128)(2,1)} %bitcast.25), kind=kLoop, calls=%fused_computation.8 | loop fusion | flops 73726 | bytes 110592
  15.4 2.7 %collective-permute-done.2 = bf16[4,144,128]{2,1,0:T(8,128)(2,1)S(1)} collective-permute-done((bf16[4,144,128]{2,1,0:T(8,128)(2,1)S(1)}, bf16[4,144,128]{2,1,0:T(8,128)(2,1)S(1)}, u32[]{:S(2)}, u32[]{:S(2)}) %collective-permute-start.2) | collective-permute-done | bytes 147488 | tf_op jit(solution)/shard_map/ppermute | solution.py:221
  18.1 1.8 %collective-permute-start.3 = (bf16[8,144,128]{2,1,0:T(8,128)(2,1)S(1)}, bf16[8,144,128]{2,1,0:T(8,128)(2,1)S(1)}, u32[]{:S(2)}, u32[]{:S(2)}) collective-permute-start(bf16[8,144,128]{2,1,0:T(8,128)(2,1)S(1)} %pad_maximum_fusion), channel_id=1, source_target_pairs={{0,2},{1,3},{2,0},{3,1},{4,6},{5,7},{6,4},{7,5},{8,10},{9,11},{10,... | collective-permute-start | bytes 884744 | tf_op jit(solution)/shard_map/ppermute | solution.py:221
  20.0 0.0 copy-start
  20.0 0.0 copy-start.1
  20.0 0.0 copy-start.2
  20.0 0.0 copy-start.3
  20.0 0.0 copy-start.4
  20.0 0.1 constant_dynamic-update-slice_fusion.1
  20.1 4.8 %collective-permute-done.3 = bf16[8,144,128]{2,1,0:T(8,128)(2,1)S(1)} collective-permute-done((bf16[8,144,128]{2,1,0:T(8,128)(2,1)S(1)}, bf16[8,144,128]{2,1,0:T(8,128)(2,1)S(1)}, u32[]{:S(2)}, u32[]{:S(2)}) %collective-permute-start.3) | collective-permute-done | bytes 294944 | tf_op jit(solution)/shard_map/ppermute | solution.py:221
  24.9 0.1 constant_dynamic-update-slice_fusion
  25.0 0.1 collective-permute-start.4
  25.1 2.0 %collective-permute-done.4 = bf16[16,144,128]{2,1,0:T(8,128)(2,1)S(1)} collective-permute-done((bf16[16,144,128]{2,1,0:T(8,128)(2,1)S(1)}, bf16[16,144,128]{2,1,0:T(8,128)(2,1)S(1)}, u32[]{:S(2)}, u32[]{:S(2)}) %collective-permute-start.4) | collective-permute-done | bytes 589856 | tf_op jit(solution)/shard_map/ppermute | solution.py:221
  27.1 0.1 constant_dynamic-update-slice_fusion.5.g_ref
  27.2 0.0 copy-done
  27.2 0.0 copy-done.1
  27.2 0.0 copy-done.2
  27.2 0.0 copy-done.3
  27.2 0.0 copy-done.4
  27.2 12.5 %sketch_gram.1 = (bf16[2048,128]{1,0:T(8,128)(2,1)S(1)}, bf16[2048,128]{1,0:T(8,128)(2,1)S(1)}, f32[128,128]{1,0:T(8,128)S(1)}) custom-call(bf16[4,64,128,128]{3,2,1,0:T(8,128)(2,1)} %bitcast.23, s32[4,64]{1,0:T(4,128)S(1)} %bitcast.19, s32[4,64]{1,0:T(4,128)S(1)} %bitcast.20, s32[4]{0:T(128)S(1)} %bitcast.22, s32[4,64]{1,0:T(4,128)S(1)} %bitcast.21, ...), custom_call_target="tpu_custom_call" | custom-call | tf_op jit(solution)/shard_map/sketch_gram/pallas_call | solution.py:123
  39.8 13.5 %all_to_all.10 = f32[32,4,128]{2,1,0:T(4,128)S(1)} all-to-all(f32[32,4,128]{2,1,0:T(4,128)S(1)} %bitcast.17), channel_id=1, replica_groups=mesh['rows'=8,'blk'=4] {'rows','blk'}, dimensions={0} | all-to-all | bytes 131072 | tf_op jit(solution)/shard_map/all_to_all | solution.py:232
  53.4 9.1 %all_to_all.11 = f32[32,4,128]{2,1,0:T(4,128)S(1)} all-to-all(f32[32,4,128]{2,1,0:T(4,128)S(1)} %broadcast_in_dim.13), channel_id=1, replica_groups=mesh['rows'=8,'blk'=4] {'rows','blk'}, dimensions={0} | all-to-all | bytes 131072 | tf_op jit(solution)/shard_map/all_to_all | solution.py:234
  62.5 7.8 %cholesky_basis.1 = (f32[2048,128]{1,0:T(8,128)}, f32[128,128]{1,0:T(8,128)}) custom-call(f32[128,128]{1,0:T(8,128)S(1)} %bitcast.16, bf16[2048,128]{1,0:T(8,128)(2,1)S(1)} %get-tuple-element.8.hi_ref, bf16[2048,128]{1,0:T(8,128)(2,1)S(1)} %get-tuple-element.9.lo_ref), custom_call_target="tpu_custom_call" | custom-call | tf_op jit(solution)/shard_map/cholesky_basis/pallas_call | solution.py:193
  (9 shorter events, 0.2 us)
Async XLA Ops:
  2.1 6.4 %collective-permute-start = (bf16[1,144,128]{2,1,0:T(8,128)(2,1)S(1)}, bf16[1,144,128]{2,1,0:T(8,128)(2,1)S(1)}, u32[]{:S(2)}, u32[]{:S(2)}) collective-permute-start(bf16[1,144,128]{2,1,0:T(8,128)(2,1)S(1)} %maximum_bitcast_fusion), channel_id=1, source_target_pairs={{0,16},{1,17},{2,18},{3,19},{4,20},{5,21},{6,22},{7,23},{8,24},{9,... | collective-permute-start | bytes 110600 | tf_op jit(solution)/shard_map/ppermute | solution.py:221
  8.4 4.4 %collective-permute-start.1 = (bf16[2,144,128]{2,1,0:T(8,128)(2,1)S(1)}, bf16[2,144,128]{2,1,0:T(8,128)(2,1)S(1)}, u32[]{:S(2)}, u32[]{:S(2)}) collective-permute-start(bf16[2,144,128]{2,1,0:T(8,128)(2,1)S(1)} %pad_maximum_fusion.2), channel_id=1, source_target_pairs={{0,8},{1,9},{2,10},{3,11},{4,12},{5,13},{6,14},{7,15},{8,0},{9,1},... | collective-permute-start | bytes 221192 | tf_op jit(solution)/shard_map/ppermute | solution.py:221
  12.9 5.2 %collective-permute-start.2 = (bf16[4,144,128]{2,1,0:T(8,128)(2,1)S(1)}, bf16[4,144,128]{2,1,0:T(8,128)(2,1)S(1)}, u32[]{:S(2)}, u32[]{:S(2)}) collective-permute-start(bf16[4,144,128]{2,1,0:T(8,128)(2,1)S(1)} %pad_maximum_fusion.1), channel_id=1, source_target_pairs={{0,4},{1,5},{2,6},{3,7},{4,0},{5,1},{6,2},{7,3},{8,12},{9,13},{10,... | collective-permute-start | bytes 442376 | tf_op jit(solution)/shard_map/ppermute | solution.py:221
  18.1 6.8 %collective-permute-start.3 = (bf16[8,144,128]{2,1,0:T(8,128)(2,1)S(1)}, bf16[8,144,128]{2,1,0:T(8,128)(2,1)S(1)}, u32[]{:S(2)}, u32[]{:S(2)}) collective-permute-start(bf16[8,144,128]{2,1,0:T(8,128)(2,1)S(1)} %pad_maximum_fusion), channel_id=1, source_target_pairs={{0,2},{1,3},{2,0},{3,1},{4,6},{5,7},{6,4},{7,5},{8,10},{9,11},{10,... | collective-permute-start | bytes 884744 | tf_op jit(solution)/shard_map/ppermute | solution.py:221
  20.0 7.2 %copy-start = (f32[1,1,2048]{2,1,0:T(1,128)S(1)}, f32[1,1,2048]{2,1,0:T(1,128)}, u32[]{:S(2)}) copy-start(f32[1,1,2048]{2,1,0:T(1,128)} %param.13) | copy-start | bytes 24580
  20.0 7.2 %copy-start.1 = (s32[1,1,4,64]{3,2,1,0:T(4,128)S(1)}, s32[1,1,4,64]{3,2,1,0:T(4,128)}, u32[]{:S(2)}) copy-start(s32[1,1,4,64]{3,2,1,0:T(4,128)} %param.9) | copy-start | bytes 3076
  20.0 7.2 %copy-start.2 = (s32[1,1,4,64]{3,2,1,0:T(4,128)S(1)}, s32[1,1,4,64]{3,2,1,0:T(4,128)}, u32[]{:S(2)}) copy-start(s32[1,1,4,64]{3,2,1,0:T(4,128)} %param.10) | copy-start | bytes 3076
  20.0 7.2 %copy-start.3 = (s32[1,1,4,64]{3,2,1,0:T(4,128)S(1)}, s32[1,1,4,64]{3,2,1,0:T(4,128)}, u32[]{:S(2)}) copy-start(s32[1,1,4,64]{3,2,1,0:T(4,128)} %param.12) | copy-start | bytes 3076
  20.0 7.2 %copy-start.4 = (s32[1,1,4]{2,1,0:T(1,128)S(1)}, s32[1,1,4]{2,1,0:T(1,128)}, u32[]{:S(2)}) copy-start(s32[1,1,4]{2,1,0:T(1,128)} %param.11) | copy-start | bytes 52
  25.0 2.1 %collective-permute-start.4 = (bf16[16,144,128]{2,1,0:T(8,128)(2,1)S(1)}, bf16[16,144,128]{2,1,0:T(8,128)(2,1)S(1)}, u32[]{:S(2)}, u32[]{:S(2)}) collective-permute-start(bf16[16,144,128]{2,1,0:T(8,128)(2,1)S(1)} %get-tuple-element.12), channel_id=1, source_target_pairs={{0,1},{1,0},{2,3},{3,2},{4,5},{5,4},{6,7},{7,6},{8,9},{9,8},{10,11... | collective-permute-start | bytes 1769480 | tf_op jit(solution)/shard_map/ppermute | solution.py:221

commit v2 on v1

v2 whole, which is shorter than its diff:
```python
import functools
import math

import jax
import jax.numpy as jnp
from jax import lax
from jax.experimental import pallas as pl
from jax.experimental.pallas import tpu as pltpu
from jax.sharding import PartitionSpec as P

SCALE = 16.0
MOST_SAMPLES = 8
GROUP = 16
DEPTH = 4
PAD = 16
SMEM = pl.BlockSpec(memory_space=pltpu.SMEM)
VMEM = pl.BlockSpec(memory_space=pltpu.VMEM)


def piece_kernel(test_hbm, deg_hbm, out_ref, deg_ref, sem, deg_sem):
    n = test_hbm.shape[0]
    rows = pltpu.make_async_copy(test_hbm, out_ref.at[0, pl.ds(0, n)], sem)
    degs = pltpu.make_async_copy(deg_hbm, deg_ref, deg_sem)
    rows.start()
    degs.start()
    degs.wait()
    rest = jnp.broadcast_to(deg_ref[...], (PAD, deg_ref.shape[1]))
    at = lax.broadcasted_iota(jnp.int32, rest.shape, 0)
    out = jnp.zeros_like(rest)
    for i in range(3):
        h = rest.astype(jnp.bfloat16).astype(jnp.float32)
        out = jnp.where(at == i, h, out)
        rest = rest - h
    out_ref[0, n:n + PAD, :] = out.astype(jnp.bfloat16)
    rows.wait()


def make_piece(test, deg):
    n, width = test.shape
    HBM = pl.BlockSpec(memory_space=pltpu.HBM)
    return pl.pallas_call(
        piece_kernel,
        out_shape=jax.ShapeDtypeStruct((1, n + PAD, width), jnp.bfloat16),
        in_specs=[HBM, HBM],
        out_specs=VMEM,
        scratch_shapes=[pltpu.VMEM((1, width), jnp.float32), pltpu.SemaphoreType.DMA, pltpu.SemaphoreType.DMA],
        compiler_params=pltpu.CompilerParams(vmem_limit_bytes=2 << 20),
        name="piece",
    )(pltpu.with_memory_space_constraint(test, pltpu.HBM), pltpu.with_memory_space_constraint(deg, pltpu.HBM))


def logs_kernel(slabs, first, place, *refs):
    w_hbm, rd_hbm, row_hbm, col_hbm, samp_hbm, cnt_hbm = refs[:6]
    refs = refs[7:]
    if not first:
        _, was_s, list_s = refs[:3]
        refs = refs[3:]
        x_ref, cur_s, tile_s = refs[:3]
        refs = refs[3:]
    else:
        x_ref, cur_s, tile_s, off_s = refs[:4]
        refs = refs[4:]
    wbuf, rd_ref, rb_ref, row_ref, row_s, col_s, samp_s, cnt_s, sem, small, inv_s, tab_s = refs
    n_slabs, cap = w_hbm.shape[:2]
    bands, n = rd_ref.shape
    blocks = x_ref.shape[0]
    zero, trash = blocks - 2, blocks - 1
    chunks = cap // GROUP

    def copy(s, c):
        return pltpu.make_async_copy(w_hbm.at[s, pl.ds(c * GROUP, GROUP)],
                                     wbuf.at[s - slabs[0], pl.ds(c * GROUP, GROUP)], sem.at[s - slabs[0], c])

    pairs = [(cnt_hbm, cnt_s), (rd_hbm, rd_ref), (row_hbm, row_s), (col_hbm, col_s), (samp_hbm, samp_s)]
    if first:
        pairs.append((row_hbm, row_ref))
    smalls = [pltpu.make_async_copy(p, r, small.at[i]) for i, (p, r) in enumerate(pairs)]
    for c in smalls:
        c.start()
    copy(slabs[0], 0).start()
    if first:
        x_ref[zero] = jnp.full((n, n), -1e30, jnp.float32)
    else:
        for q in range(bands):
            cur_s[q] = was_s[q]
        def keep(i, carry):
            tile_s[i] = list_s[i]
            return carry
        lax.fori_loop(0, zero, keep, 0, unroll=16)
    tile_s[zero] = 0
    for j in range(1, MOST_SAMPLES + 1):
        inv_s[j] = jnp.float32(1.0 / j)
    base, by_col, by_slab = place
    for c, v in enumerate(by_col):
        tab_s[c] = v ^ base() if base else v
    smalls[0].wait()
    for s in slabs:
        for c in range(chunks):
            if (s, c) != (slabs[0], 0):
                @pl.when(c * GROUP < cnt_s[s])
                def _():
                    copy(s, c).start()
    smalls[1].wait()
    for q in range(bands):
        rb_ref[q] = jnp.transpose(jnp.broadcast_to(SCALE / rd_ref[q:q + 1, :], (n, n)))
    for c in smalls[2:]:
        c.wait()
    if first:
        rows = row_ref[...]
        slab = lax.broadcasted_iota(jnp.int32, rows.shape, 0)
        lane = lax.broadcasted_iota(jnp.int32, rows.shape, 1)
        live = jnp.zeros(rows.shape, jnp.int32)
        for s in range(n_slabs):
            live = jnp.where(slab == s, cnt_s[s], live)
        rows = jnp.where(lane < live, rows, bands)
        off_s[0] = 0
        cur_s[0] = 0
        for q in range(1, bands + 1):
            p = jnp.sum(jnp.where(rows < q, 1.0, 0.0)).astype(jnp.int32)
            off_s[q] = p
            if q < bands:
                cur_s[q] = p

    for s in slabs:
        live = cnt_s[s]
        def chunk(c, carry):
            copy(s, c).wait()
            todo = []
            for j in range(GROUP):
                k = c * GROUP + j
                ok = k < live
                q = row_s[s, k]
                p = cur_s[q]
                cur_s[q] = p + ok.astype(jnp.int32)
                dest = jnp.where(ok, p, trash)
                tile_s[dest] = tab_s[col_s[s, k]] ^ by_slab[s]
                todo.append((k, q, dest, inv_s[samp_s[s, k]]))
            for k, q, dest, sc in todo:
                x_ref[dest] = jnp.log((wbuf[s - slabs[0], k].astype(jnp.float32) * sc) * rb_ref[q])
            return carry
        lax.fori_loop(0, (live + GROUP - 1) // GROUP, chunk, 0)


def block_logs(w, rd, rows, cols, samples, counts, held, slabs, place, state=None):
    n_slabs, cap, n, _ = w.shape
    bands = rd.shape[0]
    blocks = n_slabs * cap + 2
    first = state is None
    out = [jax.ShapeDtypeStruct((blocks, n, n), jnp.float32), jax.ShapeDtypeStruct((bands,), jnp.int32),
           jax.ShapeDtypeStruct((blocks,), jnp.int32)]
    if first:
        out.append(jax.ShapeDtypeStruct((bands + 1,), jnp.int32))
    HBM = pl.BlockSpec(memory_space=pltpu.HBM)
    ins = [pltpu.with_memory_space_constraint(v, pltpu.HBM) for v in (w, rd, rows, cols, samples, counts)]
    return pl.pallas_call(
        functools.partial(logs_kernel, slabs, first, place),
        out_shape=out,
        in_specs=[HBM] * 6 + [pl.BlockSpec(memory_space=pl.ANY)] + ([] if first else [VMEM, SMEM, SMEM]),
        out_specs=[VMEM] + [SMEM] * (len(out) - 1),
        scratch_shapes=[
            pltpu.VMEM((len(slabs), cap, n, n), jnp.bfloat16),
            pltpu.VMEM((bands, n), jnp.float32),
            pltpu.VMEM((bands, n, n), jnp.float32),
            pltpu.VMEM(rows.shape, jnp.int32),
            pltpu.SMEM(rows.shape, jnp.int32),
            pltpu.SMEM(rows.shape, jnp.int32),
            pltpu.SMEM(rows.shape, jnp.int32),
            pltpu.SMEM(counts.shape, jnp.int32),
            pltpu.SemaphoreType.DMA((len(slabs), cap // GROUP)),
            pltpu.SemaphoreType.DMA((6,)),
            pltpu.SMEM((MOST_SAMPLES + 1,), jnp.float32),
            pltpu.SMEM((len(place[1]),), jnp.int32),
        ],
        input_output_aliases={} if first else {7: 0},
        compiler_params=pltpu.CompilerParams(vmem_limit_bytes=10 << 20),
        cost_estimate=pl.CostEstimate(flops=0, bytes_accessed=len(slabs) * cap * n * n * 4, transcendentals=0),
        name="block_logs",
    )(*ins, held, *(state[:3] if state else ()))


def products_kernel(x_ref, off_s, tile_s, *refs):
    hi_ref, lo_ref, gram_ref, g_ref, lc_ref, acc_ref = refs[-6:]
    n = x_ref.shape[-1]
    bands = off_s.shape[0] - 1
    zero = x_ref.shape[0] - 2
    most = off_s[1] - off_s[0]
    for q in range(1, bands):
        most = jnp.maximum(most, off_s[q + 1] - off_s[q])

    at = 0
    for part in refs[:-6]:
        for i in range(part.shape[0]):
            g_ref[at] = part[i, 0:n, :]
            d = part[i, n:n + PAD, :].astype(jnp.float32)
            lc_ref[at] = jnp.broadcast_to(jnp.log(d[0:1] + d[1:2] + d[2:3]), (8, n))
            at += 1
    acc_ref[...] = jnp.zeros_like(acc_ref)

    def step(it, carry):
        for q in range(bands):
            e, t = [], []
            for j in range(DEPTH):
                i = off_s[q] + (it * DEPTH + j)
                i = jnp.where(i < off_s[q + 1], i, zero)
                l = tile_s[i]
                y = x_ref[i].reshape(n // 8, 8, n) - lc_ref[l][None]
                e.append(jnp.maximum(y, 0.0).reshape(n, n).astype(jnp.bfloat16))
                t.append(g_ref[l])
            acc_ref[q] += jnp.dot(jnp.concatenate(e, axis=1), jnp.concatenate(t, axis=0),
                                  preferred_element_type=jnp.float32)
        return carry
    lax.fori_loop(0, (most + DEPTH - 1) // DEPTH, step, 0)

    gram = jnp.zeros((n, 2 * n), jnp.float32)
    for q in range(bands):
        a = acc_ref[q]
        h = a.astype(jnp.bfloat16)
        l = (a - h.astype(jnp.float32)).astype(jnp.bfloat16)
        hi_ref[q * n:(q + 1) * n, :] = h
        lo_ref[q * n:(q + 1) * n, :] = l
        gram = gram + lax.dot_general(h, jnp.concatenate([h, l], axis=1), (((0,), (0,)), ((), ())),
                                      preferred_element_type=jnp.float32)
    cross = gram[:, n:]
    gram_ref[...] = gram[:, :n] + (cross + jnp.transpose(cross))


def products(x, off, tiles, parts):
    n = x.shape[-1]
    bands = off.shape[0] - 1
    total = sum(p.shape[0] for p in parts)
    return pl.pallas_call(
        products_kernel,
        out_shape=(jax.ShapeDtypeStruct((bands * n, n), jnp.bfloat16), jax.ShapeDtypeStruct((bands * n, n), jnp.bfloat16),
                   jax.ShapeDtypeStruct((n, n), jnp.float32)),
        in_specs=[VMEM, SMEM, SMEM] + [VMEM] * len(parts),
        out_specs=(VMEM, VMEM, VMEM),
        scratch_shapes=[
            pltpu.VMEM((total, n, n), jnp.bfloat16),
            pltpu.VMEM((total, 8, n), jnp.float32),
            pltpu.VMEM((bands, n, n), jnp.float32),
        ],
        compiler_params=pltpu.CompilerParams(vmem_limit_bytes=8 << 20),
        name="products_gram",
    )(x, off, tiles, *parts)


def _rep(x, n):
    return jnp.broadcast_to(x, (1, n))

def split(x):
    h = x.astype(jnp.bfloat16)
    x = x - h.astype(jnp.float32)
    m = x.astype(jnp.bfloat16)
    return h, m, (x - m.astype(jnp.float32)).astype(jnp.bfloat16)


def stacked_gram(a, b):
    ah, am, al = split(a)
    bh, bm, bl = split(b)
    return lax.dot_general(jnp.concatenate([ah, ah, am, am, ah, al], axis=0),
                           jnp.concatenate([bh, bm, bh, bm, bl, bh], axis=0),
                           (((0,), (0,)), ((), ())), preferred_element_type=jnp.float32)


def solve_kernel(nb, root, chunk, gram_ref, hi_ref, lo_ref, basis_ref, tri_ref, m_ref, u_ref):
    n = gram_ref.shape[0]
    ii = lax.broadcasted_iota(jnp.int32, (n, n), 0)
    jj = lax.broadcasted_iota(jnp.int32, (n, n), 1)
    m_ref[:, :n] = gram_ref[...]
    m_ref[:, n:] = (ii == jj).astype(jnp.float32)
    for r0 in range(0, n, nb):
        panel = m_ref[r0:r0 + nb, :]
        left = [panel[t:t + 1, :n] for t in range(nb)]
        right = [panel[t:t + 1, n:] for t in range(nb)]
        s = [[_rep(panel[t:t + 1, r0 + u:r0 + u + 1], n) if u >= t else None for u in range(nb)] for t in range(nb)]
        for t in range(nb):
            r = lax.rsqrt(s[t][t])
            left[t] = left[t] * r
            right[t] = right[t] * r
            f = [s[t][u] * r if u > t else None for u in range(nb)]
            for u in range(t + 1, nb):
                left[u] = left[u] - f[u] * left[t]
                right[u] = right[u] - f[u] * right[t]
                for v in range(u, nb):
                    s[u][v] = s[u][v] - f[u] * f[v]
        u_l = jnp.concatenate(left, axis=0)
        u_r = jnp.concatenate(right, axis=0)
        u_ref[r0:r0 + nb, :n] = u_l
        u_ref[r0:r0 + nb, n:] = u_r
        if r0 + nb < n:
            upd = stacked_gram(u_l, jnp.concatenate([u_l, u_r], axis=1))
            m_ref[r0 + nb:, :] = m_ref[r0 + nb:, :] - upd[r0 + nb:, :]
    tri_ref[...] = jnp.where(jj >= ii, u_ref[:, :n], 0.0) * (1.0 / root)
    w = jnp.where(jj <= ii, u_ref[:, n:], 0.0) * root
    wh = w.astype(jnp.bfloat16)
    wl = (w - wh.astype(jnp.float32)).astype(jnp.bfloat16)
    both = jnp.concatenate([wh, wl], axis=0)
    dims = (((1,), (1,)), ((), ()))
    for c in range(0, hi_ref.shape[0], chunk):
        h = hi_ref[c:c + chunk, :]
        l = lo_ref[c:c + chunk, :]
        a = lax.dot_general(h, both, dims, preferred_element_type=jnp.float32)
        b = lax.dot_general(l, wh, dims, preferred_element_type=jnp.float32)
        basis_ref[c:c + chunk, :] = a[:, :n] + (a[:, n:] + b)

def solve(gram, hi, lo, root, nb=16, chunk=256):
    n = gram.shape[0]
    V = pl.BlockSpec(memory_space=pltpu.VMEM)
    return pl.pallas_call(
        functools.partial(solve_kernel, nb, root, chunk),
        out_shape=(jax.ShapeDtypeStruct(hi.shape, jnp.float32), jax.ShapeDtypeStruct((n, n), jnp.float32)),
        in_specs=[V, V, V], out_specs=(V, V),
        scratch_shapes=[pltpu.VMEM((n, 2 * n), jnp.float32), pltpu.VMEM((n, 2 * n), jnp.float32)],
        compiler_params=pltpu.CompilerParams(vmem_limit_bytes=6 << 20),
        name="cholesky_basis",
    )(gram, hi, lo)


AXES = ("rows", "blk")


def send(x, mask, n_dev):
    return lax.ppermute(x, AXES, [(i, i ^ mask) for i in range(n_dev)])


def sum_all(x, n_dev):
    width = min(x.shape[1], x.size // n_dev)
    shares = x.reshape(n_dev, -1, width)
    mine = lax.all_to_all(shares, AXES, 0, 0, tiled=True).sum(axis=0)
    sent = jnp.broadcast_to(mine[None], shares.shape)
    return lax.all_to_all(sent, AXES, 0, 0, tiled=True).reshape(x.shape)


def body(block_weight, block_row, block_col, block_count, block_samples, row_degree, col_degree, test_matrix):
    n_rows, n_blk = lax.axis_size("rows"), lax.axis_size("blk")
    n_dev = n_rows * n_blk
    weights = block_weight[0, 0]
    n_slabs, _, n, _ = weights.shape
    piece_len, width = test_matrix.shape[1:]
    row_deg = row_degree[0, 0].reshape(-1, n)
    me = lax.axis_index(AXES)

    if piece_len == n:
        piece = make_piece(test_matrix[0], col_degree)
    else:
        degs = jnp.broadcast_to(jnp.pad(col_degree, ((0, 0), (0, width - piece_len)), constant_values=1.0), (PAD, width))
        rows_at = lax.broadcasted_iota(jnp.int32, degs.shape, 0)
        head = jnp.zeros_like(degs)
        for i in range(3):
            h = lax.reduce_precision(degs, 8, 7)
            head = jnp.where(rows_at == i, h, head)
            degs = degs - h
        piece = jnp.concatenate([test_matrix[0], head.astype(jnp.bfloat16)], axis=0)[None]

    bits = [1 << i for i in range(1, n_dev.bit_length() - 1)]
    plane, line = bits[:2], bits[2:][::-1]
    masks = [0, plane[0], plane[1], plane[0] ^ plane[1]]
    group = jnp.concatenate([piece] + [send(piece, m, n_dev) for m in masks[1:]], axis=0)
    parts = [group]
    half = n_slabs // 2
    slab_sets = [range(half), range(half, n_slabs)]
    order = list(masks)
    for m in line:
        order = order + [v ^ m for v in order]
    order = order + [v ^ 1 for v in order]
    n_cols = n_rows * piece_len // n
    if piece_len == n:
        weights_of = [order.index(1 << i) for i in range(n_dev.bit_length() - 1)]
        spread = lambda v: sum(w for i, w in enumerate(weights_of) if v >> i & 1)
        def base():
            at = lax.axis_index("rows") * n_blk + lax.axis_index("blk")
            return sum(((at >> i) & 1) * w for i, w in enumerate(weights_of))
        place = (base, [spread(c * n_blk) for c in range(n_cols)], [spread(s) for s in range(n_blk)])
    else:
        place = (None, [c * n_blk for c in range(n_cols)], list(range(n_blk)))
    tables = (row_deg, block_row[0, 0], block_col[0, 0], block_samples[0, 0], block_count[0, 0])
    state = None
    swapped = []
    for step, m in enumerate(line):
        got = send(group, m, n_dev)
        swapped.append(send(parts[-1], 1, n_dev))
        if step >= len(line) - 2:
            slabs = slab_sets[step - (len(line) - 2)]
            state = [*block_logs(weights, *tables, group, slabs, place, state), *(state or [])[3:]]
            got, *state = lax.optimization_barrier((got, *state))
        parts.append(got)
        group = jnp.concatenate([group, got], axis=0)
    swapped.append(send(parts[-1], 1, n_dev))
    parts = parts + swapped
    if piece_len != n:
        share = n // piece_len
        pieces = jnp.concatenate(parts, axis=0)[jnp.argsort(me ^ jnp.asarray(order, jnp.int32))]
        pieces = pieces.reshape(n_rows // share, share, n_blk, piece_len + PAD, width).transpose(0, 2, 1, 3, 4)
        pieces = pieces.reshape(-1, share, piece_len + PAD, width)
        tiles = pieces[:, :, :piece_len].reshape(-1, n, width)
        heads = pieces[:, :, piece_len:, :piece_len].transpose(0, 2, 1, 3).reshape(-1, PAD, n)
        parts = [jnp.concatenate([tiles, heads], axis=1)]
    hi, lo, gram = products(state[0], state[3], state[2], parts)
    gram = sum_all(gram, n_dev)
    basis, triangle = solve(gram, hi, lo, math.sqrt(hi.shape[0] * n_dev))
    return basis[None, None], triangle


def solution(mesh):
    placed = (
        P("rows", "blk", None, None, None, None),
        P("rows", "blk", None, None),
        P("rows", "blk", None, None),
        P("rows", "blk", None),
        P("rows", "blk", None, None),
        P("rows", "blk", None),
        P("blk", "rows"),
        P("blk", "rows", None),
    )
    return jax.shard_map(
        body,
        mesh=mesh,
        in_specs=placed,
        out_specs=(P("rows", "blk", None, None), P()),
        check_vma=False,
    )
```

time: 70.4 us -> 60.1 us (0.85)
  waiting for transfers between devices: 14.6 us -> 9.27 us
  other arithmetic: 2.32 us -> 0.06 us
  blocking collectives: 22.6 us -> 20.7 us
  starting transfers between devices: 9.25 us -> 8.48 us
    ppermute x5 -> x8, waiting for transfers between devices: 14.6 us -> 9.27 us  [send(): return lax.ppermute(x, AXES, [(i, i ^ mask) for i in range(n_dev)])]
    all_to_all x1, blocking collectives: 13.5 us -> 11.6 us  [sum_all(): mine = lax.all_to_all(shares, AXES, 0, 0, tiled=True).sum(axis=0)]
    pallas_call x1 -> x4, Pallas kernels: 12.5 us -> 14 us  [the longest x2 8.37 us: block_logs(): pl.pallas_call(functools.partial(logs_kernel, slabs, first, place), out_s...]
    pallas_call x1, Pallas kernels: 7.75 us -> 6.45 us  [solve(): pl.pallas_call(functools.partial(solve_kernel, nb, root, chunk), out_shap...]
    ppermute x5 -> x8, starting transfers between devices: 9.25 us -> 8.48 us  [send(): return lax.ppermute(x, AXES, [(i, i ^ mask) for i in range(n_dev)])]
    unnamed x1 -> x0, other arithmetic: 0.77 us -> none
    broadcast_in_dim x1 -> x0, other arithmetic: 0.76 us -> none  [gather_pieces(): got = piece[None]]
  transfers between devices with their start and end apart: 5 -> 8, of which waited for: 5 -> 7; matrix products, arithmetic and copies ran while one was open for 1% -> 0% of each run, Pallas kernels for 0% -> 14%
where the time goes in v2:
time: 60.1 us; the launch traced here: 59.7 us
  blocking collectives  20.7 us (34%)
  Pallas kernels  20.4 us (34%)
  waiting for transfers between devices  9.27 us (15%)
  starting transfers between devices  8.48 us (14%)
  between operations  0.69 us (1%)
    all_to_all x1, blocking collectives, sum_all(): mine = lax.all_to_all(shares, AXES, 0, 0, tiled=True).sum(axis=0)  11.6 us
    ppermute x8, waiting for transfers between devices, send(): return lax.ppermute(x, AXES, [(i, i ^ mask) for i in range(n_dev)])  9.27 us
    all_to_all x1, blocking collectives, sum_all(): return lax.all_to_all(sent, AXES, 0, 0, tiled=True).reshape(x.shape)  9.1 us
    ppermute x8, starting transfers between devices, send(): return lax.ppermute(x, AXES, [(i, i ^ mask) for i in range(n_dev)])  8.48 us
    pallas_call x2, Pallas kernels, block_logs(): pl.pallas_call(functools.partial(logs_kernel, slabs, first, place), out_s...  8.37 us
    pallas_call x1, Pallas kernels, solve(): pl.pallas_call(functools.partial(solve_kernel, nb, root, chunk), out_shap...  6.45 us
    pallas_call x1, Pallas kernels, products(): pl.pallas_call(products_kernel, out_shape=(jax.ShapeDtypeStruct((bands *...  4.82 us
  transfers between devices with their start and end apart: 8, of which 7 were waited for; matrix products, arithmetic and copies ran while one was open for 0% of the time, Pallas kernels for 14%

profile of v2, /device:TPU:0, one launch (start us, length us, event | category | flops | bytes accessed | tf_op | source)
XLA Modules:
  0.0 59.7 jit_solution(8102273641423870370)
XLA Ops:
  0.6 0.8 %piece.1 = bf16[1,144,128]{2,1,0:T(8,128)(2,1)S(1)} custom-call(bf16[128,128]{1,0:T(8,128)(2,1)} %bitcast.14, f32[1,128]{1,0:T(1,128)} %deg_hbm.1), custom_call_target="tpu_custom_call" | custom-call | tf_op jit(solution)/shard_map/piece/pallas_call | solution.py:41
  1.4 3.0 %collective-permute-start = (bf16[1,144,128]{2,1,0:T(8,128)(2,1)S(1)}, bf16[1,144,128]{2,1,0:T(8,128)(2,1)S(1)}, u32[]{:S(2)}, u32[]{:S(2)}) collective-permute-start(bf16[1,144,128]{2,1,0:T(8,128)(2,1)S(1)} %piece.1), channel_id=1, source_target_pairs={{0,2},{1,3},{2,0},{3,1},{4,6},{5,7},{6,4},{7,5},{8,10},{9,11},{10,... | collective-permute-start | bytes 110600 | tf_op jit(solution)/shard_map/ppermute | solution.py:323
  4.4 1.5 %collective-permute-start.1 = (bf16[1,144,128]{2,1,0:T(8,128)(2,1)S(1)}, bf16[1,144,128]{2,1,0:T(8,128)(2,1)S(1)}, u32[]{:S(2)}, u32[]{:S(2)}) collective-permute-start(bf16[1,144,128]{2,1,0:T(8,128)(2,1)S(1)} %piece.1), channel_id=1, source_target_pairs={{0,4},{1,5},{2,6},{3,7},{4,0},{5,1},{6,2},{7,3},{8,12},{9,13},{10,... | collective-permute-start | bytes 110600 | tf_op jit(solution)/shard_map/ppermute | solution.py:323
  5.9 0.0 collective-permute-start.2
  6.0 0.4 collective-permute-done
  6.4 2.2 %collective-permute-done.1 = bf16[1,144,128]{2,1,0:T(8,128)(2,1)S(1)} collective-permute-done((bf16[1,144,128]{2,1,0:T(8,128)(2,1)S(1)}, bf16[1,144,128]{2,1,0:T(8,128)(2,1)S(1)}, u32[]{:S(2)}, u32[]{:S(2)}) %collective-permute-start.1) | collective-permute-done | bytes 36896 | tf_op jit(solution)/shard_map/ppermute | solution.py:323
  8.5 2.3 %collective-permute-done.2 = bf16[1,144,128]{2,1,0:T(8,128)(2,1)S(1)} collective-permute-done((bf16[1,144,128]{2,1,0:T(8,128)(2,1)S(1)}, bf16[1,144,128]{2,1,0:T(8,128)(2,1)S(1)}, u32[]{:S(2)}, u32[]{:S(2)}) %collective-permute-start.2) | collective-permute-done | bytes 36896 | tf_op jit(solution)/shard_map/ppermute | solution.py:323
  10.8 2.7 %collective-permute-start.3 = (bf16[4,144,128]{2,1,0:T(8,128)(2,1)S(1)}, bf16[4,144,128]{2,1,0:T(8,128)(2,1)S(1)}, u32[]{:S(2)}, u32[]{:S(2)}) collective-permute-start(bf16[4,144,128]{2,1,0:T(8,128)(2,1)S(1)} %pad_maximum_fusion.refs_6_.refs_0_), channel_id=1, source_target_pairs={{0,16},{1,17},{2,18},{3,19},{4,20},{5,21},{6,22},{7,23},{8,24},{9,... | collective-permute-start | bytes 442376 | tf_op jit(solution)/shard_map/ppermute | solution.py:323
  13.5 4.3 %block_logs.2 = (f32[258,128,128]{2,1,0:T(8,128)S(1)}, s32[16]{0:T(128)S(1)}, s32[258]{0:T(512)S(1)}, s32[17]{0:T(128)S(1)}) custom-call(bf16[4,64,128,128]{3,2,1,0:T(8,128)(2,1)} %bitcast.12, f32[16,128]{1,0:T(8,128)} %bitcast.15, s32[4,64]{1,0:T(4,128)} %bitcast.17, s32[4,64]{1,0:T(4,128)} %bitcast.19, s32[4,64]{1,0:T(4,128)} %bitcast.21, s32[4]{0:T(128)} %bitcast.23, ...), custom_call_target="tpu_custom_call" | custom-call | bytes 8388608 | tf_op jit(solution)/shard_map/block_logs/pallas_call | solution.py:155
  17.8 1.0 %collective-permute-done.3.refs_1_ = bf16[4,144,128]{2,1,0:T(8,128)(2,1)S(1)} collective-permute-done((bf16[4,144,128]{2,1,0:T(8,128)(2,1)S(1)}, bf16[4,144,128]{2,1,0:T(8,128)(2,1)S(1)}, u32[]{:S(2)}, u32[]{:S(2)}) %collective-permute-start.3) | collective-permute-done | bytes 147488 | tf_op jit(solution)/shard_map/ppermute | solution.py:323
  18.8 0.7 %collective-permute-start.4 = (bf16[8,144,128]{2,1,0:T(8,128)(2,1)S(1)}, bf16[8,144,128]{2,1,0:T(8,128)(2,1)S(1)}, u32[]{:S(2)}, u32[]{:S(2)}) collective-permute-start(bf16[8,144,128]{2,1,0:T(8,128)(2,1)S(1)} %constant_dynamic-update-slice_fusion.refs_6_), channel_id=1, source_target_pairs={{0,8},{1,9},{2,10},{3,11},{4,12},{5,13},{6,14},{7,15},{8,0},{9,1},... | collective-permute-start | bytes 884744 | tf_op jit(solution)/shard_map/ppermute | solution.py:323
  19.6 4.1 %block_logs.3 = (f32[258,128,128]{2,1,0:T(8,128)S(1)}, s32[16]{0:T(128)}, s32[258]{0:T(512)S(1)}) custom-call(bf16[4,64,128,128]{3,2,1,0:T(8,128)(2,1)} %bitcast.13, f32[16,128]{1,0:T(8,128)} %bitcast.16, s32[4,64]{1,0:T(4,128)} %bitcast.18, s32[4,64]{1,0:T(4,128)} %bitcast.20, s32[4,64]{1,0:T(4,128)} %bitcast.22, ...), custom_call_target="tpu_custom_call", output_to_operand_aliasing={{0}: (7, {})} | custom-call | bytes 8388608 | tf_op jit(solution)/shard_map/block_logs/pallas_call | solution.py:155
  23.7 1.9 %collective-permute-done.4.refs_2_ = bf16[8,144,128]{2,1,0:T(8,128)(2,1)S(1)} collective-permute-done((bf16[8,144,128]{2,1,0:T(8,128)(2,1)S(1)}, bf16[8,144,128]{2,1,0:T(8,128)(2,1)S(1)}, u32[]{:S(2)}, u32[]{:S(2)}) %collective-permute-start.4) | collective-permute-done | bytes 294944 | tf_op jit(solution)/shard_map/ppermute | solution.py:323
  25.6 0.0 collective-permute-start.7
  25.6 0.5 collective-permute-start.5
  26.1 0.0 collective-permute-start.6
  26.2 1.3 %collective-permute-done.5.refs_3_ = bf16[4,144,128]{2,1,0:T(8,128)(2,1)S(1)} collective-permute-done((bf16[4,144,128]{2,1,0:T(8,128)(2,1)S(1)}, bf16[4,144,128]{2,1,0:T(8,128)(2,1)S(1)}, u32[]{:S(2)}, u32[]{:S(2)}) %collective-permute-start.5) | collective-permute-done | bytes 147488 | tf_op jit(solution)/shard_map/ppermute | solution.py:323
  27.4 0.2 collective-permute-done.6.refs_4_
  27.6 0.0 collective-permute-done.7.refs_5_
  27.6 4.8 %products_gram.1 = (bf16[2048,128]{1,0:T(8,128)(2,1)S(1)}, bf16[2048,128]{1,0:T(8,128)(2,1)S(1)}, f32[128,128]{1,0:T(8,128)S(1)}) custom-call(f32[258,128,128]{2,1,0:T(8,128)S(1)} %get-tuple-element.33.x_ref, s32[17]{0:T(128)S(1)} %get-tuple-element.34.off_s, s32[258]{0:T(512)S(1)} %get-tuple-element.35.tile_s, ...), custom_call_target="tpu_custom_call" | custom-call | tf_op jit(solution)/shard_map/products_gram/pallas_call | solution.py:231
  32.5 11.6 %all_to_all.10 = f32[32,4,128]{2,1,0:T(4,128)S(1)} all-to-all(f32[32,4,128]{2,1,0:T(4,128)S(1)} %bitcast.11), channel_id=1, replica_groups=mesh['rows'=8,'blk'=4] {'rows','blk'}, dimensions={0} | all-to-all | bytes 131072 | tf_op jit(solution)/shard_map/all_to_all | solution.py:329
  44.1 9.1 %all_to_all.11 = f32[32,4,128]{2,1,0:T(4,128)S(1)} all-to-all(f32[32,4,128]{2,1,0:T(4,128)S(1)} %broadcast_in_dim.4), channel_id=1, replica_groups=mesh['rows'=8,'blk'=4] {'rows','blk'}, dimensions={0} | all-to-all | bytes 131072 | tf_op jit(solution)/shard_map/all_to_all | solution.py:331
  53.2 6.4 %cholesky_basis.1 = (f32[2048,128]{1,0:T(8,128)}, f32[128,128]{1,0:T(8,128)}) custom-call(f32[128,128]{1,0:T(8,128)S(1)} %bitcast.10, bf16[2048,128]{1,0:T(8,128)(2,1)S(1)} %get-tuple-element.38.hi_ref, bf16[2048,128]{1,0:T(8,128)(2,1)S(1)} %get-tuple-element.39.lo_ref), custom_call_target="tpu_custom_call" | custom-call | tf_op jit(solution)/shard_map/cholesky_basis/pallas_call | solution.py:309
  (8 shorter events, 0.1 us)
Async XLA Ops:
  1.4 5.0 %collective-permute-start = (bf16[1,144,128]{2,1,0:T(8,128)(2,1)S(1)}, bf16[1,144,128]{2,1,0:T(8,128)(2,1)S(1)}, u32[]{:S(2)}, u32[]{:S(2)}) collective-permute-start(bf16[1,144,128]{2,1,0:T(8,128)(2,1)S(1)} %piece.1), channel_id=1, source_target_pairs={{0,2},{1,3},{2,0},{3,1},{4,6},{5,7},{6,4},{7,5},{8,10},{9,11},{10,... | collective-permute-start | bytes 110600 | tf_op jit(solution)/shard_map/ppermute | solution.py:323
  4.4 4.1 %collective-permute-start.1 = (bf16[1,144,128]{2,1,0:T(8,128)(2,1)S(1)}, bf16[1,144,128]{2,1,0:T(8,128)(2,1)S(1)}, u32[]{:S(2)}, u32[]{:S(2)}) collective-permute-start(bf16[1,144,128]{2,1,0:T(8,128)(2,1)S(1)} %piece.1), channel_id=1, source_target_pairs={{0,4},{1,5},{2,6},{3,7},{4,0},{5,1},{6,2},{7,3},{8,12},{9,13},{10,... | collective-permute-start | bytes 110600 | tf_op jit(solution)/shard_map/ppermute | solution.py:323
  5.9 4.9 %collective-permute-start.2 = (bf16[1,144,128]{2,1,0:T(8,128)(2,1)S(1)}, bf16[1,144,128]{2,1,0:T(8,128)(2,1)S(1)}, u32[]{:S(2)}, u32[]{:S(2)}) collective-permute-start(bf16[1,144,128]{2,1,0:T(8,128)(2,1)S(1)} %piece.1), channel_id=1, source_target_pairs={{0,6},{1,7},{2,4},{3,5},{4,2},{5,3},{6,0},{7,1},{8,14},{9,15},{10,... | collective-permute-start | bytes 110600 | tf_op jit(solution)/shard_map/ppermute | solution.py:323
  10.8 8.0 %collective-permute-start.3 = (bf16[4,144,128]{2,1,0:T(8,128)(2,1)S(1)}, bf16[4,144,128]{2,1,0:T(8,128)(2,1)S(1)}, u32[]{:S(2)}, u32[]{:S(2)}) collective-permute-start(bf16[4,144,128]{2,1,0:T(8,128)(2,1)S(1)} %pad_maximum_fusion.refs_6_.refs_0_), channel_id=1, source_target_pairs={{0,16},{1,17},{2,18},{3,19},{4,20},{5,21},{6,22},{7,23},{8,24},{9,... | collective-permute-start | bytes 442376 | tf_op jit(solution)/shard_map/ppermute | solution.py:323
  18.8 6.8 %collective-permute-start.4 = (bf16[8,144,128]{2,1,0:T(8,128)(2,1)S(1)}, bf16[8,144,128]{2,1,0:T(8,128)(2,1)S(1)}, u32[]{:S(2)}, u32[]{:S(2)}) collective-permute-start(bf16[8,144,128]{2,1,0:T(8,128)(2,1)S(1)} %constant_dynamic-update-slice_fusion.refs_6_), channel_id=1, source_target_pairs={{0,8},{1,9},{2,10},{3,11},{4,12},{5,13},{6,14},{7,15},{8,0},{9,1},... | collective-permute-start | bytes 884744 | tf_op jit(solution)/shard_map/ppermute | solution.py:323
  25.6 2.0 %collective-permute-start.7 = (bf16[8,144,128]{2,1,0:T(8,128)(2,1)S(1)}, bf16[8,144,128]{2,1,0:T(8,128)(2,1)S(1)}, u32[]{:S(2)}, u32[]{:S(2)}) collective-permute-start(bf16[8,144,128]{2,1,0:T(8,128)(2,1)S(1)} %collective-permute-done.4.refs_2_), channel_id=1, source_target_pairs={{0,1},{1,0},{2,3},{3,2},{4,5},{5,4},{6,7},{7,6},{8,9},{9,8},{10,11... | collective-permute-start | bytes 884744 | tf_op jit(solution)/shard_map/ppermute | solution.py:323
  25.6 1.8 %collective-permute-start.5 = (bf16[4,144,128]{2,1,0:T(8,128)(2,1)S(1)}, bf16[4,144,128]{2,1,0:T(8,128)(2,1)S(1)}, u32[]{:S(2)}, u32[]{:S(2)}) collective-permute-start(bf16[4,144,128]{2,1,0:T(8,128)(2,1)S(1)} %pad_maximum_fusion.refs_6_.refs_0_), channel_id=1, source_target_pairs={{0,1},{1,0},{2,3},{3,2},{4,5},{5,4},{6,7},{7,6},{8,9},{9,8},{10,11... | collective-permute-start | bytes 442376 | tf_op jit(solution)/shard_map/ppermute | solution.py:323
  26.1 1.5 %collective-permute-start.6 = (bf16[4,144,128]{2,1,0:T(8,128)(2,1)S(1)}, bf16[4,144,128]{2,1,0:T(8,128)(2,1)S(1)}, u32[]{:S(2)}, u32[]{:S(2)}) collective-permute-start(bf16[4,144,128]{2,1,0:T(8,128)(2,1)S(1)} %collective-permute-done.3.refs_1_), channel_id=1, source_target_pairs={{0,1},{1,0},{2,3},{3,2},{4,5},{5,4},{6,7},{7,6},{8,9},{9,8},{10,11... | collective-permute-start | bytes 442376 | tf_op jit(solution)/shard_map/ppermute | solution.py:323

commit v3 on v2

--- a/solution.py
+++ b/solution.py
@@ -12,6 +12,8 @@
 MOST_SAMPLES = 8
 GROUP = 16
 DEPTH = 4
+ITEMS = (32, 16)
+PLACES = 1 << 16
 PAD = 16
 SMEM = pl.BlockSpec(memory_space=pltpu.SMEM)
 VMEM = pl.BlockSpec(memory_space=pltpu.VMEM)
@@ -53,16 +55,16 @@
     w_hbm, rd_hbm, row_hbm, col_hbm, samp_hbm, cnt_hbm = refs[:6]
     refs = refs[7:]
     if not first:
-        _, was_s, list_s = refs[:3]
-        refs = refs[3:]
+        _, was_s, list_s, rb_ref = refs[:4]
+        refs = refs[4:]
         x_ref, cur_s, tile_s = refs[:3]
         refs = refs[3:]
     else:
-        x_ref, cur_s, tile_s, off_s = refs[:4]
-        refs = refs[4:]
-    wbuf, rd_ref, rb_ref, row_ref, row_s, col_s, samp_s, cnt_s, sem, small, inv_s, tab_s = refs
+        x_ref, cur_s, tile_s, rb_ref, off_s, item_s = refs[:6]
+        refs = refs[6:]
+    wbuf, rd_ref, row_ref, row_s, col_s, samp_s, cnt_s, sem, small, inv_s, tab_s = refs
     n_slabs, cap = w_hbm.shape[:2]
-    bands, n = rd_ref.shape
+    bands, n = rb_ref.shape[:2]
     blocks = x_ref.shape[0]
     zero, trash = blocks - 2, blocks - 1
     chunks = cap // GROUP
@@ -71,9 +73,9 @@
         return pltpu.make_async_copy(w_hbm.at[s, pl.ds(c * GROUP, GROUP)],
                                      wbuf.at[s - slabs[0], pl.ds(c * GROUP, GROUP)], sem.at[s - slabs[0], c])
 
-    pairs = [(cnt_hbm, cnt_s), (rd_hbm, rd_ref), (row_hbm, row_s), (col_hbm, col_s), (samp_hbm, samp_s)]
+    pairs = [(cnt_hbm, cnt_s), (row_hbm, row_s), (col_hbm, col_s), (samp_hbm, samp_s)]
     if first:
-        pairs.append((row_hbm, row_ref))
+        pairs += [(rd_hbm, rd_ref), (row_hbm, row_ref)]
     smalls = [pltpu.make_async_copy(p, r, small.at[i]) for i, (p, r) in enumerate(pairs)]
     for c in smalls:
         c.start()
@@ -100,12 +102,11 @@
                 @pl.when(c * GROUP < cnt_s[s])
                 def _():
                     copy(s, c).start()
-    smalls[1].wait()
-    for q in range(bands):
-        rb_ref[q] = jnp.transpose(jnp.broadcast_to(SCALE / rd_ref[q:q + 1, :], (n, n)))
-    for c in smalls[2:]:
+    for c in smalls[1:]:
         c.wait()
     if first:
+        for q in range(bands):
+            rb_ref[q] = jnp.transpose(jnp.broadcast_to(SCALE / rd_ref[q:q + 1, :], (n, n)))
         rows = row_ref[...]
         slab = lax.broadcasted_iota(jnp.int32, rows.shape, 0)
         lane = lax.broadcasted_iota(jnp.int32, rows.shape, 1)
@@ -120,6 +121,17 @@
             off_s[q] = p
             if q < bands:
                 cur_s[q] = p
+        rounds = item_s.shape[0] // bands - 2
+        starts = [off_s[q] for q in range(bands + 1)]
+        count = jnp.int32(0)
+        for it in range(rounds):
+            for q in range(bands):
+                first_at = starts[q] + it * DEPTH
+                item_s[count] = q * PLACES + first_at
+                count = count + (first_at < starts[q + 1]).astype(jnp.int32)
+        for i in range(ITEMS[0]):
+            item_s[count + i] = PLACES - 1 - DEPTH
+        off_s[bands + 1] = count
 
     for s in slabs:
         live = cnt_s[s]
@@ -149,18 +161,19 @@
     out = [jax.ShapeDtypeStruct((blocks, n, n), jnp.float32), jax.ShapeDtypeStruct((bands,), jnp.int32),
            jax.ShapeDtypeStruct((blocks,), jnp.int32)]
     if first:
-        out.append(jax.ShapeDtypeStruct((bands + 1,), jnp.int32))
+        rounds = -(-n_slabs * len(place[1]) // DEPTH)
+        out += [jax.ShapeDtypeStruct((bands, n, n), jnp.float32), jax.ShapeDtypeStruct((bands + 2,), jnp.int32),
+                jax.ShapeDtypeStruct(((rounds + 2) * bands,), jnp.int32)]
     HBM = pl.BlockSpec(memory_space=pltpu.HBM)
     ins = [pltpu.with_memory_space_constraint(v, pltpu.HBM) for v in (w, rd, rows, cols, samples, counts)]
     return pl.pallas_call(
         functools.partial(logs_kernel, slabs, first, place),
         out_shape=out,
-        in_specs=[HBM] * 6 + [pl.BlockSpec(memory_space=pl.ANY)] + ([] if first else [VMEM, SMEM, SMEM]),
-        out_specs=[VMEM] + [SMEM] * (len(out) - 1),
+        in_specs=[HBM] * 6 + [pl.BlockSpec(memory_space=pl.ANY)] + ([] if first else [VMEM, SMEM, SMEM, VMEM]),
+        out_specs=[VMEM, SMEM, SMEM] + ([VMEM, SMEM, SMEM] if first else []),
         scratch_shapes=[
             pltpu.VMEM((len(slabs), cap, n, n), jnp.bfloat16),
             pltpu.VMEM((bands, n), jnp.float32),
-            pltpu.VMEM((bands, n, n), jnp.float32),
             pltpu.VMEM(rows.shape, jnp.int32),
             pltpu.SMEM(rows.shape, jnp.int32),
             pltpu.SMEM(rows.shape, jnp.int32),
@@ -172,20 +185,17 @@
             pltpu.SMEM((len(place[1]),), jnp.int32),
         ],
         input_output_aliases={} if first else {7: 0},
-        compiler_params=pltpu.CompilerParams(vmem_limit_bytes=10 << 20),
+        compiler_params=pltpu.CompilerParams(vmem_limit_bytes=12 << 20),
         cost_estimate=pl.CostEstimate(flops=0, bytes_accessed=len(slabs) * cap * n * n * 4, transcendentals=0),
         name="block_logs",
-    )(*ins, held, *(state[:3] if state else ()))
-
-
-def products_kernel(x_ref, off_s, tile_s, *refs):
+    )(*ins, held, *(state[:4] if state else ()))
+
+
+def products_kernel(x_ref, off_s, item_s, tile_s, *refs):
     hi_ref, lo_ref, gram_ref, g_ref, lc_ref, acc_ref = refs[-6:]
     n = x_ref.shape[-1]
-    bands = off_s.shape[0] - 1
+    bands = off_s.shape[0] - 2
     zero = x_ref.shape[0] - 2
-    most = off_s[1] - off_s[0]
-    for q in range(1, bands):
-        most = jnp.maximum(most, off_s[q + 1] - off_s[q])
 
     at = 0
     for part in refs[:-6]:
@@ -196,20 +206,29 @@
             at += 1
     acc_ref[...] = jnp.zeros_like(acc_ref)
 
-    def step(it, carry):
-        for q in range(bands):
-            e, t = [], []
-            for j in range(DEPTH):
-                i = off_s[q] + (it * DEPTH + j)
-                i = jnp.where(i < off_s[q + 1], i, zero)
-                l = tile_s[i]
-                y = x_ref[i].reshape(n // 8, 8, n) - lc_ref[l][None]
-                e.append(jnp.maximum(y, 0.0).reshape(n, n).astype(jnp.bfloat16))
-                t.append(g_ref[l])
-            acc_ref[q] += jnp.dot(jnp.concatenate(e, axis=1), jnp.concatenate(t, axis=0),
-                                  preferred_element_type=jnp.float32)
-        return carry
-    lax.fori_loop(0, (most + DEPTH - 1) // DEPTH, step, 0)
+    def step(first, items):
+        def run(it, carry):
+            for k in range(items):
+                word = item_s[first + it * items + k]
+                q = word >> 16
+                last = off_s[q + 1]
+                e, t = [], []
+                for j in range(DEPTH):
+                    i = (word & (PLACES - 1)) + j
+                    i = jnp.where(i < last, i, zero)
+                    l = tile_s[i]
+                    y = x_ref[i].reshape(n // 8, 8, n) - lc_ref[l][None]
+                    e.append(jnp.maximum(y, 0.0).reshape(n, n).astype(jnp.bfloat16))
+                    t.append(g_ref[l])
+                acc_ref[q] += jnp.dot(jnp.concatenate(e, axis=1), jnp.concatenate(t, axis=0),
+                                      preferred_element_type=jnp.float32)
+            return carry
+        return run
+    long, short = ITEMS
+    count = off_s[bands + 1]
+    longs = (count + long - short - 1) // long
+    lax.fori_loop(0, longs, step(0, long), 0)
+    lax.fori_loop(0, (jnp.maximum(count - longs * long, 0) + short - 1) // short, step(longs * long, short), 0)
 
     gram = jnp.zeros((n, 2 * n), jnp.float32)
     for q in range(bands):
@@ -224,15 +243,15 @@
     gram_ref[...] = gram[:, :n] + (cross + jnp.transpose(cross))
 
 
-def products(x, off, tiles, parts):
+def products(x, off, items, tiles, parts):
     n = x.shape[-1]
-    bands = off.shape[0] - 1
+    bands = off.shape[0] - 2
     total = sum(p.shape[0] for p in parts)
     return pl.pallas_call(
         products_kernel,
         out_shape=(jax.ShapeDtypeStruct((bands * n, n), jnp.bfloat16), jax.ShapeDtypeStruct((bands * n, n), jnp.bfloat16),
                    jax.ShapeDtypeStruct((n, n), jnp.float32)),
-        in_specs=[VMEM, SMEM, SMEM] + [VMEM] * len(parts),
+        in_specs=[VMEM, SMEM, SMEM, SMEM] + [VMEM] * len(parts),
         out_specs=(VMEM, VMEM, VMEM),
         scratch_shapes=[
             pltpu.VMEM((total, n, n), jnp.bfloat16),
@@ -241,7 +260,7 @@
         ],
         compiler_params=pltpu.CompilerParams(vmem_limit_bytes=8 << 20),
         name="products_gram",
-    )(x, off, tiles, *parts)
+    )(x, off, items, tiles, *parts)
 
 
 def _rep(x, n):
@@ -254,44 +273,44 @@
     return h, m, (x - m.astype(jnp.float32)).astype(jnp.bfloat16)
 
 
-def stacked_gram(a, b):
-    ah, am, al = split(a)
-    bh, bm, bl = split(b)
-    return lax.dot_general(jnp.concatenate([ah, ah, am, am, ah, al], axis=0),
-                           jnp.concatenate([bh, bm, bh, bm, bl, bh], axis=0),
+def stacked_gram(x):
+    h, m, l = split(x)
+    return lax.dot_general(jnp.concatenate([h, h, m, m, h, l], axis=0), jnp.concatenate([h, m, h, m, l, h], axis=0),
                            (((0,), (0,)), ((), ())), preferred_element_type=jnp.float32)
 
 
-def solve_kernel(nb, root, chunk, gram_ref, hi_ref, lo_ref, basis_ref, tri_ref, m_ref, u_ref):
+def solve_kernel(nb, root, chunk, gram_ref, hi_ref, lo_ref, basis_ref, tri_ref, m_ref):
     n = gram_ref.shape[0]
+    lane = lax.broadcasted_iota(jnp.int32, (1, n), 1)
+    m_ref[...] = gram_ref[...]
+    for r0 in range(0, n, nb):
+        panel = m_ref[r0:r0 + nb, :]
+        s = [[_rep(panel[t:t + 1, r0 + u:r0 + u + 1], n) if u >= t else None for u in range(nb)] for t in range(nb)]
+        inside = (lane >= r0) & (lane < r0 + nb)
+        rows = [jnp.where(inside, jnp.where(lane == r0 + t, 1.0, 0.0), panel[t:t + 1, :]) for t in range(nb)]
+        tops = []
+        for t in range(nb):
+            r = lax.rsqrt(s[t][t])
+            rows[t] = rows[t] * r
+            f = [s[t][u] * r if u >= t else None for u in range(nb)]
+            for u in range(t + 1, nb):
+                rows[u] = rows[u] - f[u] * rows[t]
+                for v in range(u, nb):
+                    s[u][v] = s[u][v] - f[u] * f[v]
+            top = rows[t]
+            for u in range(t, nb):
+                top = jnp.where(lane == r0 + u, f[u], top)
+            tops.append(top)
+        x = jnp.concatenate(rows, axis=0)
+        tri_ref[r0:r0 + nb, :] = jnp.concatenate(tops, axis=0)
+        m_ref[r0:r0 + nb, :] = x
+        if r0 + nb < n:
+            below = m_ref[r0 + nb:, :]
+            m_ref[r0 + nb:, :] = jnp.where(inside, 0.0, below) - stacked_gram(x)[r0 + nb:, :]
     ii = lax.broadcasted_iota(jnp.int32, (n, n), 0)
     jj = lax.broadcasted_iota(jnp.int32, (n, n), 1)
-    m_ref[:, :n] = gram_ref[...]
-    m_ref[:, n:] = (ii == jj).astype(jnp.float32)
-    for r0 in range(0, n, nb):
-        panel = m_ref[r0:r0 + nb, :]
-        left = [panel[t:t + 1, :n] for t in range(nb)]
-        right = [panel[t:t + 1, n:] for t in range(nb)]
-        s = [[_rep(panel[t:t + 1, r0 + u:r0 + u + 1], n) if u >= t else None for u in range(nb)] for t in range(nb)]
-        for t in range(nb):
-            r = lax.rsqrt(s[t][t])
-            left[t] = left[t] * r
-            right[t] = right[t] * r
-            f = [s[t][u] * r if u > t else None for u in range(nb)]
-            for u in range(t + 1, nb):
-                left[u] = left[u] - f[u] * left[t]
-                right[u] = right[u] - f[u] * right[t]
-                for v in range(u, nb):
-                    s[u][v] = s[u][v] - f[u] * f[v]
-        u_l = jnp.concatenate(left, axis=0)
-        u_r = jnp.concatenate(right, axis=0)
-        u_ref[r0:r0 + nb, :n] = u_l
-        u_ref[r0:r0 + nb, n:] = u_r
-        if r0 + nb < n:
-            upd = stacked_gram(u_l, jnp.concatenate([u_l, u_r], axis=1))
-            m_ref[r0 + nb:, :] = m_ref[r0 + nb:, :] - upd[r0 + nb:, :]
-    tri_ref[...] = jnp.where(jj >= ii, u_ref[:, :n], 0.0) * (1.0 / root)
-    w = jnp.where(jj <= ii, u_ref[:, n:], 0.0) * root
+    tri_ref[...] = jnp.where(jj >= ii, tri_ref[...], 0.0) * (1.0 / root)
+    w = jnp.where(jj <= ii, m_ref[...], 0.0) * root
     wh = w.astype(jnp.bfloat16)
     wl = (w - wh.astype(jnp.float32)).astype(jnp.bfloat16)
     both = jnp.concatenate([wh, wl], axis=0)
@@ -303,20 +322,22 @@
         b = lax.dot_general(l, wh, dims, preferred_element_type=jnp.float32)
         basis_ref[c:c + chunk, :] = a[:, :n] + (a[:, n:] + b)
 
-def solve(gram, hi, lo, root, nb=16, chunk=256):
+
+def solve(gram, hi, lo, root, nb=16, chunk=512):
     n = gram.shape[0]
     V = pl.BlockSpec(memory_space=pltpu.VMEM)
     return pl.pallas_call(
         functools.partial(solve_kernel, nb, root, chunk),
         out_shape=(jax.ShapeDtypeStruct(hi.shape, jnp.float32), jax.ShapeDtypeStruct((n, n), jnp.float32)),
         in_specs=[V, V, V], out_specs=(V, V),
-        scratch_shapes=[pltpu.VMEM((n, 2 * n), jnp.float32), pltpu.VMEM((n, 2 * n), jnp.float32)],
+        scratch_shapes=[pltpu.VMEM((n, n), jnp.float32)],
         compiler_params=pltpu.CompilerParams(vmem_limit_bytes=6 << 20),
         name="cholesky_basis",
     )(gram, hi, lo)
 
 
 AXES = ("rows", "blk")
+STAGES = ((0, 1), (1, 2), (0, 0), (2, 4))
 
 
 def send(x, mask, n_dev):
@@ -353,15 +374,11 @@
         piece = jnp.concatenate([test_matrix[0], head.astype(jnp.bfloat16)], axis=0)[None]
 
     bits = [1 << i for i in range(1, n_dev.bit_length() - 1)]
-    plane, line = bits[:2], bits[2:][::-1]
-    masks = [0, plane[0], plane[1], plane[0] ^ plane[1]]
-    group = jnp.concatenate([piece] + [send(piece, m, n_dev) for m in masks[1:]], axis=0)
-    parts = [group]
-    half = n_slabs // 2
-    slab_sets = [range(half), range(half, n_slabs)]
-    order = list(masks)
+    line, plane = bits[2:][::-1], (bits[0], bits[1], bits[0] ^ bits[1])
+    order = [0]
     for m in line:
         order = order + [v ^ m for v in order]
+    order = [v ^ m for m in (0, *plane) for v in order]
     order = order + [v ^ 1 for v in order]
     n_cols = n_rows * piece_len // n
     if piece_len == n:
@@ -374,18 +391,34 @@
     else:
         place = (None, [c * n_blk for c in range(n_cols)], list(range(n_blk)))
     tables = (row_deg, block_row[0, 0], block_col[0, 0], block_samples[0, 0], block_count[0, 0])
-    state = None
-    swapped = []
+    slab_sets = [range(n_slabs * a // 4, n_slabs * b // 4) for a, b in STAGES]
+
+    def logs(state, held, stage):
+        if not len(slab_sets[stage]):
+            return state
+        return [*block_logs(weights, *tables, held, slab_sets[stage], place, state), *(state or [])[3:]]
+
+    group, state = piece, None
     for step, m in enumerate(line):
         got = send(group, m, n_dev)
-        swapped.append(send(parts[-1], 1, n_dev))
-        if step >= len(line) - 2:
-            slabs = slab_sets[step - (len(line) - 2)]
-            state = [*block_logs(weights, *tables, group, slabs, place, state), *(state or [])[3:]]
-            got, *state = lax.optimization_barrier((got, *state))
-        parts.append(got)
+        stage = step - (len(line) - 2)
+        if stage >= 0:
+            state = logs(state, group, stage)
+            if state:
+                got, *state = lax.optimization_barrier((got, *state))
         group = jnp.concatenate([group, got], axis=0)
-    swapped.append(send(parts[-1], 1, n_dev))
+    one, two = plane[:2]
+    near = send(group, two, n_dev)
+    side = send(group, one, n_dev)
+    swapped = send(group, 1, n_dev)
+    state = logs(state, group, 2)
+    near, *state = lax.optimization_barrier((near, *state))
+    far = send(near, one, n_dev)
+    near_swapped = send(near, 1, n_dev)
+    state = logs(state, near, 3)
+    side, far, swapped, near_swapped, state[0] = lax.optimization_barrier((side, far, swapped, near_swapped, state[0]))
+    parts = [group, side, near, far]
+    swapped = [swapped, send(side, 1, n_dev), near_swapped, send(far, 1, n_dev)]
     parts = parts + swapped
     if piece_len != n:
         share = n // piece_len
@@ -395,7 +428,7 @@
         tiles = pieces[:, :, :piece_len].reshape(-1, n, width)
         heads = pieces[:, :, piece_len:, :piece_len].transpose(0, 2, 1, 3).reshape(-1, PAD, n)
         parts = [jnp.concatenate([tiles, heads], axis=1)]
-    hi, lo, gram = products(state[0], state[3], state[2], parts)
+    hi, lo, gram = products(state[0], state[4], state[5], state[2], parts)
     gram = sum_all(gram, n_dev)
     basis, triangle = solve(gram, hi, lo, math.sqrt(hi.shape[0] * n_dev))
     return basis[None, None], triangle

time: 60.1 us -> 57.3 us (0.953)
  waiting for transfers between devices: 9.27 us -> 3.33 us
  starting transfers between devices: 8.48 us -> 11.5 us
    ppermute x8 -> x9, waiting for transfers between devices: 9.27 us -> 3.33 us  [send(): return lax.ppermute(x, AXES, [(i, i ^ mask) for i in range(n_dev)])]
    ppermute x8 -> x9, starting transfers between devices: 8.48 us -> 11.5 us  [send(): return lax.ppermute(x, AXES, [(i, i ^ mask) for i in range(n_dev)])]
    pallas_call x2 -> x3, Pallas kernels: 8.37 us -> 10.2 us  [block_logs(): pl.pallas_call(functools.partial(logs_kernel, slabs, first, place), out_s...]
    pallas_call x1, Pallas kernels: 4.82 us -> 3.28 us  [products(): pl.pallas_call(products_kernel, out_shape=(jax.ShapeDtypeStruct((bands *...]
  transfers between devices with their start and end apart: 8 -> 9, of which waited for: 7 -> 3; matrix products, arithmetic and copies ran while one was open for 0% -> 0% of each run, Pallas kernels for 14% -> 18%
where the time goes in v3:
time: 57.3 us; the launch traced here: 57.2 us
  blocking collectives  20.9 us (36%)
  Pallas kernels  20.6 us (36%)
  starting transfers between devices  11.5 us (20%)
  waiting for transfers between devices  3.33 us (6%)
  between operations  0.74 us (1%)
    all_to_all x1, blocking collectives, sum_all(): mine = lax.all_to_all(shares, AXES, 0, 0, tiled=True).sum(axis=0)  11.8 us
    ppermute x9, starting transfers between devices, send(): return lax.ppermute(x, AXES, [(i, i ^ mask) for i in range(n_dev)])  11.5 us
    pallas_call x3, Pallas kernels, block_logs(): pl.pallas_call(functools.partial(logs_kernel, slabs, first, place), out_s...  10.2 us
    all_to_all x1, blocking collectives, sum_all(): return lax.all_to_all(sent, AXES, 0, 0, tiled=True).reshape(x.shape)  9.1 us
    pallas_call x1, Pallas kernels, solve(): pl.pallas_call(functools.partial(solve_kernel, nb, root, chunk), out_shap...  6.31 us
    ppermute x9, waiting for transfers between devices, send(): return lax.ppermute(x, AXES, [(i, i ^ mask) for i in range(n_dev)])  3.33 us
    pallas_call x1, Pallas kernels, products(): pl.pallas_call(products_kernel, out_shape=(jax.ShapeDtypeStruct((bands *...  3.28 us
  transfers between devices with their start and end apart: 9, of which 3 were waited for; matrix products, arithmetic and copies ran while one was open for 0% of the time, Pallas kernels for 18%

profile of v3, /device:TPU:0, one launch (start us, length us, event | category | flops | bytes accessed | tf_op | source)
XLA Modules:
  0.0 57.2 jit_solution(17630252529216340227)
XLA Ops:
  0.6 0.8 %piece.1.refs_6_ = bf16[1,144,128]{2,1,0:T(8,128)(2,1)S(1)} custom-call(bf16[128,128]{1,0:T(8,128)(2,1)} %bitcast.18, f32[1,128]{1,0:T(1,128)} %deg_hbm.1), custom_call_target="tpu_custom_call" | custom-call | tf_op jit(solution)/shard_map/piece/pallas_call | solution.py:43
  1.4 4.1 %collective-permute-start = (bf16[1,144,128]{2,1,0:T(8,128)(2,1)S(1)}, bf16[1,144,128]{2,1,0:T(8,128)(2,1)S(1)}, u32[]{:S(2)}, u32[]{:S(2)}) collective-permute-start(bf16[1,144,128]{2,1,0:T(8,128)(2,1)S(1)} %piece.1.refs_6_), channel_id=1, source_target_pairs={{0,16},{1,17},{2,18},{3,19},{4,20},{5,21},{6,22},{7,23},{8,24},{9,... | collective-permute-start | bytes 110600 | tf_op jit(solution)/shard_map/ppermute | solution.py:344
  5.5 2.9 %block_logs.3 = (f32[258,128,128]{2,1,0:T(8,128)S(1)}, s32[16]{0:T(128)S(1)}, s32[258]{0:T(512)S(1)}, f32[16,128,128]{2,1,0:T(8,128)S(1)}, s32[18]{0:T(128)S(1)}, /*index=5*/s32[160]{0:T(256)S(1)}) custom-call(bf16[4,64,128,128]{3,2,1,0:T(8,128)(2,1)} %bitcast.12, f32[16,128]{1,0:T(8,128)} %bitcast.15, s32[4,64]{1,0:T(4,128)} %bitcast.19, s32[4,64]{1,0:T(4,128)} %bitcast.22, ...), custom_call_target="tpu_custom_call" | custom-call | bytes 4194304 | tf_op jit(solution)/shard_map/block_logs/pallas_call | solution.py:169
  8.5 0.0 collective-permute-done
  8.5 1.4 %collective-permute-start.1 = (bf16[2,144,128]{2,1,0:T(8,128)(2,1)S(1)}, bf16[2,144,128]{2,1,0:T(8,128)(2,1)S(1)}, u32[]{:S(2)}, u32[]{:S(2)}) collective-permute-start(bf16[2,144,128]{2,1,0:T(8,128)(2,1)S(1)} %pad_maximum_fusion.1.refs_6_), channel_id=1, source_target_pairs={{0,8},{1,9},{2,10},{3,11},{4,12},{5,13},{6,14},{7,15},{8,0},{9,1},... | collective-permute-start | bytes 221192 | tf_op jit(solution)/shard_map/ppermute | solution.py:344
  9.9 3.2 %block_logs.4 = (f32[258,128,128]{2,1,0:T(8,128)S(1)}, s32[16]{0:T(128)S(1)}, s32[258]{0:T(512)S(1)}) custom-call(bf16[4,64,128,128]{3,2,1,0:T(8,128)(2,1)} %bitcast.13, f32[16,128]{1,0:T(8,128)} %bitcast.16, s32[4,64]{1,0:T(4,128)} %bitcast.20, s32[4,64]{1,0:T(4,128)} %bitcast.23, s32[4,64]{1,0:T(4,128)} %bitcast.26, ...), custom_call_target="tpu_custom_call", output_to_operand_aliasing={{0}: (7, {})} | custom-call | bytes 4194304 | tf_op jit(solution)/shard_map/block_logs/pallas_call | solution.py:169
  13.2 0.0 collective-permute-done.1
  13.2 2.3 %collective-permute-start.3 = (bf16[4,144,128]{2,1,0:T(8,128)(2,1)S(1)}, bf16[4,144,128]{2,1,0:T(8,128)(2,1)S(1)}, u32[]{:S(2)}, u32[]{:S(2)}) collective-permute-start(bf16[4,144,128]{2,1,0:T(8,128)(2,1)S(1)} %pad_maximum_fusion.refs_0_), channel_id=1, source_target_pairs={{0,4},{1,5},{2,6},{3,7},{4,0},{5,1},{6,2},{7,3},{8,12},{9,13},{10,... | collective-permute-start | bytes 442376 | tf_op jit(solution)/shard_map/ppermute | solution.py:344
  15.5 1.3 %collective-permute-start.2 = (bf16[4,144,128]{2,1,0:T(8,128)(2,1)S(1)}, bf16[4,144,128]{2,1,0:T(8,128)(2,1)S(1)}, u32[]{:S(2)}, u32[]{:S(2)}) collective-permute-start(bf16[4,144,128]{2,1,0:T(8,128)(2,1)S(1)} %pad_maximum_fusion.refs_0_), channel_id=1, source_target_pairs={{0,2},{1,3},{2,0},{3,1},{4,6},{5,7},{6,4},{7,5},{8,10},{9,11},{10,... | collective-permute-start | bytes 442376 | tf_op jit(solution)/shard_map/ppermute | solution.py:344
  16.7 0.0 collective-permute-start.5
  16.8 2.0 %collective-permute-done.3.refs_6_.refs_2_ = bf16[4,144,128]{2,1,0:T(8,128)(2,1)S(1)} collective-permute-done((bf16[4,144,128]{2,1,0:T(8,128)(2,1)S(1)}, bf16[4,144,128]{2,1,0:T(8,128)(2,1)S(1)}, u32[]{:S(2)}, u32[]{:S(2)}) %collective-permute-start.3) | collective-permute-done | bytes 147488 | tf_op jit(solution)/shard_map/ppermute | solution.py:344
  18.8 1.5 %collective-permute-start.4 = (bf16[4,144,128]{2,1,0:T(8,128)(2,1)S(1)}, bf16[4,144,128]{2,1,0:T(8,128)(2,1)S(1)}, u32[]{:S(2)}, u32[]{:S(2)}) collective-permute-start(bf16[4,144,128]{2,1,0:T(8,128)(2,1)S(1)} %collective-permute-done.3.refs_6_.refs_2_), channel_id=1, source_target_pairs={{0,2},{1,3},{2,0},{3,1},{4,6},{5,7},{6,4},{7,5},{8,10},{9,11},{10,... | collective-permute-start | bytes 442376 | tf_op jit(solution)/shard_map/ppermute | solution.py:344
  20.3 0.0 collective-permute-start.6
  20.3 4.0 %block_logs.5 = (f32[258,128,128]{2,1,0:T(8,128)S(1)}, s32[16]{0:T(128)}, s32[258]{0:T(512)S(1)}) custom-call(bf16[4,64,128,128]{3,2,1,0:T(8,128)(2,1)} %bitcast.14, f32[16,128]{1,0:T(8,128)} %bitcast.17, s32[4,64]{1,0:T(4,128)} %bitcast.21, s32[4,64]{1,0:T(4,128)} %bitcast.24, s32[4,64]{1,0:T(4,128)} %bitcast.27, ...), custom_call_target="tpu_custom_call", output_to_operand_aliasing={{0}: (7, {})} | custom-call | bytes 8388608 | tf_op jit(solution)/shard_map/block_logs/pallas_call | solution.py:169
  24.4 0.0 collective-permute-done.2.refs_1_
  24.4 0.0 collective-permute-done.5.refs_4_
  24.4 0.0 collective-permute-done.4.refs_3_
  24.4 0.0 collective-permute-done.6.refs_6_
  24.4 0.8 %collective-permute-start.7 = (bf16[4,144,128]{2,1,0:T(8,128)(2,1)S(1)}, bf16[4,144,128]{2,1,0:T(8,128)(2,1)S(1)}, u32[]{:S(2)}, u32[]{:S(2)}) collective-permute-start(bf16[4,144,128]{2,1,0:T(8,128)(2,1)S(1)} %collective-permute-done.2.refs_1_), channel_id=1, source_target_pairs={{0,1},{1,0},{2,3},{3,2},{4,5},{5,4},{6,7},{7,6},{8,9},{9,8},{10,11... | collective-permute-start | bytes 442376 | tf_op jit(solution)/shard_map/ppermute | solution.py:344
  25.2 0.1 collective-permute-start.8
  25.3 0.9 %collective-permute-done.7.refs_5_ = bf16[4,144,128]{2,1,0:T(8,128)(2,1)S(1)} collective-permute-done((bf16[4,144,128]{2,1,0:T(8,128)(2,1)S(1)}, bf16[4,144,128]{2,1,0:T(8,128)(2,1)S(1)}, u32[]{:S(2)}, u32[]{:S(2)}) %collective-permute-start.7) | collective-permute-done | bytes 147488 | tf_op jit(solution)/shard_map/ppermute | solution.py:344
  26.2 0.4 collective-permute-done.8.refs_7_
  26.6 3.3 %products_gram.1 = (bf16[2048,128]{1,0:T(8,128)(2,1)S(1)}, bf16[2048,128]{1,0:T(8,128)(2,1)S(1)}, f32[128,128]{1,0:T(8,128)S(1)}) custom-call(f32[258,128,128]{2,1,0:T(8,128)S(1)} %get-tuple-element.73.x_ref, s32[18]{0:T(128)S(1)} %get-tuple-element.74.off_s, s32[160]{0:T(256)S(1)} %get-tuple-element.75.item_s, s32[258]{0:T(512)S(1)} %get-tuple-element.76.tile_s, ...), custom_call_target="tpu_custom_call" | custom-call | tf_op jit(solution)/shard_map/products_gram/pallas_call | solution.py:250
  29.9 11.8 %all_to_all.10 = f32[32,4,128]{2,1,0:T(4,128)S(1)} all-to-all(f32[32,4,128]{2,1,0:T(4,128)S(1)} %bitcast.11), channel_id=1, replica_groups=mesh['rows'=8,'blk'=4] {'rows','blk'}, dimensions={0} | all-to-all | bytes 131072 | tf_op jit(solution)/shard_map/all_to_all | solution.py:350
  41.8 9.1 %all_to_all.11 = f32[32,4,128]{2,1,0:T(4,128)S(1)} all-to-all(f32[32,4,128]{2,1,0:T(4,128)S(1)} %broadcast_in_dim.4), channel_id=1, replica_groups=mesh['rows'=8,'blk'=4] {'rows','blk'}, dimensions={0} | all-to-all | bytes 131072 | tf_op jit(solution)/shard_map/all_to_all | solution.py:352
  50.9 6.3 %cholesky_basis.1 = (f32[2048,128]{1,0:T(8,128)}, f32[128,128]{1,0:T(8,128)}) custom-call(f32[128,128]{1,0:T(8,128)S(1)} %bitcast.10, bf16[2048,128]{1,0:T(8,128)(2,1)S(1)} %get-tuple-element.82.hi_ref, bf16[2048,128]{1,0:T(8,128)(2,1)S(1)} %get-tuple-element.83.lo_ref), custom_call_target="tpu_custom_call" | custom-call | tf_op jit(solution)/shard_map/cholesky_basis/pallas_call | solution.py:329
  (4 shorter events, 0.1 us)
Async XLA Ops:
  1.4 7.1 %collective-permute-start = (bf16[1,144,128]{2,1,0:T(8,128)(2,1)S(1)}, bf16[1,144,128]{2,1,0:T(8,128)(2,1)S(1)}, u32[]{:S(2)}, u32[]{:S(2)}) collective-permute-start(bf16[1,144,128]{2,1,0:T(8,128)(2,1)S(1)} %piece.1.refs_6_), channel_id=1, source_target_pairs={{0,16},{1,17},{2,18},{3,19},{4,20},{5,21},{6,22},{7,23},{8,24},{9,... | collective-permute-start | bytes 110600 | tf_op jit(solution)/shard_map/ppermute | solution.py:344
  8.5 4.7 %collective-permute-start.1 = (bf16[2,144,128]{2,1,0:T(8,128)(2,1)S(1)}, bf16[2,144,128]{2,1,0:T(8,128)(2,1)S(1)}, u32[]{:S(2)}, u32[]{:S(2)}) collective-permute-start(bf16[2,144,128]{2,1,0:T(8,128)(2,1)S(1)} %pad_maximum_fusion.1.refs_6_), channel_id=1, source_target_pairs={{0,8},{1,9},{2,10},{3,11},{4,12},{5,13},{6,14},{7,15},{8,0},{9,1},... | collective-permute-start | bytes 221192 | tf_op jit(solution)/shard_map/ppermute | solution.py:344
  13.2 5.6 %collective-permute-start.3 = (bf16[4,144,128]{2,1,0:T(8,128)(2,1)S(1)}, bf16[4,144,128]{2,1,0:T(8,128)(2,1)S(1)}, u32[]{:S(2)}, u32[]{:S(2)}) collective-permute-start(bf16[4,144,128]{2,1,0:T(8,128)(2,1)S(1)} %pad_maximum_fusion.refs_0_), channel_id=1, source_target_pairs={{0,4},{1,5},{2,6},{3,7},{4,0},{5,1},{6,2},{7,3},{8,12},{9,13},{10,... | collective-permute-start | bytes 442376 | tf_op jit(solution)/shard_map/ppermute | solution.py:344
  15.5 8.9 %collective-permute-start.2 = (bf16[4,144,128]{2,1,0:T(8,128)(2,1)S(1)}, bf16[4,144,128]{2,1,0:T(8,128)(2,1)S(1)}, u32[]{:S(2)}, u32[]{:S(2)}) collective-permute-start(bf16[4,144,128]{2,1,0:T(8,128)(2,1)S(1)} %pad_maximum_fusion.refs_0_), channel_id=1, source_target_pairs={{0,2},{1,3},{2,0},{3,1},{4,6},{5,7},{6,4},{7,5},{8,10},{9,11},{10,... | collective-permute-start | bytes 442376 | tf_op jit(solution)/shard_map/ppermute | solution.py:344
  16.7 7.6 %collective-permute-start.5 = (bf16[4,144,128]{2,1,0:T(8,128)(2,1)S(1)}, bf16[4,144,128]{2,1,0:T(8,128)(2,1)S(1)}, u32[]{:S(2)}, u32[]{:S(2)}) collective-permute-start(bf16[4,144,128]{2,1,0:T(8,128)(2,1)S(1)} %pad_maximum_fusion.refs_0_), channel_id=1, source_target_pairs={{0,1},{1,0},{2,3},{3,2},{4,5},{5,4},{6,7},{7,6},{8,9},{9,8},{10,11... | collective-permute-start | bytes 442376 | tf_op jit(solution)/shard_map/ppermute | solution.py:344
  18.8 5.6 %collective-permute-start.4 = (bf16[4,144,128]{2,1,0:T(8,128)(2,1)S(1)}, bf16[4,144,128]{2,1,0:T(8,128)(2,1)S(1)}, u32[]{:S(2)}, u32[]{:S(2)}) collective-permute-start(bf16[4,144,128]{2,1,0:T(8,128)(2,1)S(1)} %collective-permute-done.3.refs_6_.refs_2_), channel_id=1, source_target_pairs={{0,2},{1,3},{2,0},{3,1},{4,6},{5,7},{6,4},{7,5},{8,10},{9,11},{10,... | collective-permute-start | bytes 442376 | tf_op jit(solution)/shard_map/ppermute | solution.py:344
  20.3 4.1 %collective-permute-start.6 = (bf16[4,144,128]{2,1,0:T(8,128)(2,1)S(1)}, bf16[4,144,128]{2,1,0:T(8,128)(2,1)S(1)}, u32[]{:S(2)}, u32[]{:S(2)}) collective-permute-start(bf16[4,144,128]{2,1,0:T(8,128)(2,1)S(1)} %collective-permute-done.3.refs_6_.refs_2_), channel_id=1, source_target_pairs={{0,1},{1,0},{2,3},{3,2},{4,5},{5,4},{6,7},{7,6},{8,9},{9,8},{10,11... | collective-permute-start | bytes 442376 | tf_op jit(solution)/shard_map/ppermute | solution.py:344
  24.4 1.8 %collective-permute-start.7 = (bf16[4,144,128]{2,1,0:T(8,128)(2,1)S(1)}, bf16[4,144,128]{2,1,0:T(8,128)(2,1)S(1)}, u32[]{:S(2)}, u32[]{:S(2)}) collective-permute-start(bf16[4,144,128]{2,1,0:T(8,128)(2,1)S(1)} %collective-permute-done.2.refs_1_), channel_id=1, source_target_pairs={{0,1},{1,0},{2,3},{3,2},{4,5},{5,4},{6,7},{7,6},{8,9},{9,8},{10,11... | collective-permute-start | bytes 442376 | tf_op jit(solution)/shard_map/ppermute | solution.py:344
  25.2 1.4 %collective-permute-start.8 = (bf16[4,144,128]{2,1,0:T(8,128)(2,1)S(1)}, bf16[4,144,128]{2,1,0:T(8,128)(2,1)S(1)}, u32[]{:S(2)}, u32[]{:S(2)}) collective-permute-start(bf16[4,144,128]{2,1,0:T(8,128)(2,1)S(1)} %collective-permute-done.4.refs_3_), channel_id=1, source_target_pairs={{0,1},{1,0},{2,3},{3,2},{4,5},{5,4},{6,7},{7,6},{8,9},{9,8},{10,11... | collective-permute-start | bytes 442376 | tf_op jit(solution)/shard_map/ppermute | solution.py:344

commit v4 on v3

--- a/solution.py
+++ b/solution.py
@@ -263,9 +263,6 @@
     )(x, off, items, tiles, *parts)
 
 
-def _rep(x, n):
-    return jnp.broadcast_to(x, (1, n))
-
 def split(x):
     h = x.astype(jnp.bfloat16)
     x = x - h.astype(jnp.float32)
@@ -273,10 +270,9 @@
     return h, m, (x - m.astype(jnp.float32)).astype(jnp.bfloat16)
 
 
-def stacked_gram(x):
+def stacked(x):
     h, m, l = split(x)
-    return lax.dot_general(jnp.concatenate([h, h, m, m, h, l], axis=0), jnp.concatenate([h, m, h, m, l, h], axis=0),
-                           (((0,), (0,)), ((), ())), preferred_element_type=jnp.float32)
+    return jnp.concatenate([h, h, m, m, h, l], axis=0).T, jnp.concatenate([h, m, h, m, l, h], axis=0)
 
 
 def solve_kernel(nb, root, chunk, gram_ref, hi_ref, lo_ref, basis_ref, tri_ref, m_ref):
@@ -285,28 +281,30 @@
     m_ref[...] = gram_ref[...]
     for r0 in range(0, n, nb):
         panel = m_ref[r0:r0 + nb, :]
-        s = [[_rep(panel[t:t + 1, r0 + u:r0 + u + 1], n) if u >= t else None for u in range(nb)] for t in range(nb)]
+        sub = lax.broadcasted_iota(jnp.int32, (nb, n), 0)
         inside = (lane >= r0) & (lane < r0 + nb)
-        rows = [jnp.where(inside, jnp.where(lane == r0 + t, 1.0, 0.0), panel[t:t + 1, :]) for t in range(nb)]
-        tops = []
+        eye = jnp.where(lax.broadcasted_iota(jnp.int32, (nb, n), 1) == sub + r0, 1.0, 0.0)
+        c = [jnp.broadcast_to(panel[:, r0 + v:r0 + v + 1], (nb, n)) for v in range(nb)]
+        x = jnp.where(inside, eye, panel)
+        scale = jnp.zeros((nb, n), jnp.float32)
         for t in range(nb):
-            r = lax.rsqrt(s[t][t])
-            rows[t] = rows[t] * r
-            f = [s[t][u] * r if u >= t else None for u in range(nb)]
-            for u in range(t + 1, nb):
-                rows[u] = rows[u] - f[u] * rows[t]
-                for v in range(u, nb):
-                    s[u][v] = s[u][v] - f[u] * f[v]
-            top = rows[t]
-            for u in range(t, nb):
-                top = jnp.where(lane == r0 + u, f[u], top)
-            tops.append(top)
-        x = jnp.concatenate(rows, axis=0)
-        tri_ref[r0:r0 + nb, :] = jnp.concatenate(tops, axis=0)
+            r = lax.rsqrt(c[t][t:t + 1, :])
+            f = c[t] * r
+            fm = jnp.where(sub > t, f, 0.0)
+            for v in range(t + 1, nb):
+                c[v] = c[v] - fm * f[v:v + 1, :]
+            row = x[t:t + 1, :] * r
+            x = jnp.where(sub == t, row, x - fm * row)
+            scale = jnp.where(sub == t, r, scale)
+        top = x
+        for v in range(nb):
+            top = jnp.where(lane == r0 + v, c[v] * scale, top)
+        tri_ref[r0:r0 + nb, :] = top
         m_ref[r0:r0 + nb, :] = x
         if r0 + nb < n:
-            below = m_ref[r0 + nb:, :]
-            m_ref[r0 + nb:, :] = jnp.where(inside, 0.0, below) - stacked_gram(x)[r0 + nb:, :]
+            lhs, rhs = stacked(x)
+            below = jnp.where(inside, 0.0, m_ref[r0 + nb:, :])
+            m_ref[r0 + nb:, :] = below - jnp.dot(lhs[r0 + nb:], rhs, preferred_element_type=jnp.float32)
     ii = lax.broadcasted_iota(jnp.int32, (n, n), 0)
     jj = lax.broadcasted_iota(jnp.int32, (n, n), 1)
     tri_ref[...] = jnp.where(jj >= ii, tri_ref[...], 0.0) * (1.0 / root)
@@ -323,7 +321,7 @@
         basis_ref[c:c + chunk, :] = a[:, :n] + (a[:, n:] + b)
 
 
-def solve(gram, hi, lo, root, nb=16, chunk=512):
+def solve(gram, hi, lo, root, nb=16, chunk=256):
     n = gram.shape[0]
     V = pl.BlockSpec(memory_space=pltpu.VMEM)
     return pl.pallas_call(

time: 57.3 us -> 56.1 us (0.979)
  Pallas kernels: 20.6 us -> 19.5 us
  blocking collectives: 20.9 us -> 20 us
    pallas_call x1, Pallas kernels: 6.31 us -> 4.94 us  [solve(): pl.pallas_call(functools.partial(solve_kernel, nb, root, chunk), out_shap...]
    all_to_all x1, blocking collectives: 11.8 us -> 10.9 us  [sum_all(): mine = lax.all_to_all(shares, AXES, 0, 0, tiled=True).sum(axis=0)]
  transfers between devices with their start and end apart: 9 -> 9, of which waited for: 3 -> 3; matrix products, arithmetic and copies ran while one was open for 0% -> 0% of each run, Pallas kernels for 18% -> 19%
where the time goes in v4:
time: 56.1 us; the launch traced here: 55.7 us
  blocking collectives  20 us (36%)
  Pallas kernels  19.5 us (35%)
  starting transfers between devices  11.7 us (21%)
  waiting for transfers between devices  3.69 us (7%)
  between operations  0.74 us (1%)
    ppermute x9, starting transfers between devices, send(): return lax.ppermute(x, AXES, [(i, i ^ mask) for i in range(n_dev)])  11.7 us
    all_to_all x1, blocking collectives, sum_all(): mine = lax.all_to_all(shares, AXES, 0, 0, tiled=True).sum(axis=0)  10.9 us
    pallas_call x3, Pallas kernels, block_logs(): pl.pallas_call(functools.partial(logs_kernel, slabs, first, place), out_s...  10.5 us
    all_to_all x1, blocking collectives, sum_all(): return lax.all_to_all(sent, AXES, 0, 0, tiled=True).reshape(x.shape)  9.1 us
    pallas_call x1, Pallas kernels, solve(): pl.pallas_call(functools.partial(solve_kernel, nb, root, chunk), out_shap...  4.94 us
    ppermute x9, waiting for transfers between devices, send(): return lax.ppermute(x, AXES, [(i, i ^ mask) for i in range(n_dev)])  3.69 us
    pallas_call x1, Pallas kernels, products(): pl.pallas_call(products_kernel, out_shape=(jax.ShapeDtypeStruct((bands *...  3.27 us
  transfers between devices with their start and end apart: 9, of which 3 were waited for; matrix products, arithmetic and copies ran while one was open for 0% of the time, Pallas kernels for 19%

profile of v4, /device:TPU:0, one launch (start us, length us, event | category | flops | bytes accessed | tf_op | source)
XLA Modules:
  0.0 55.7 jit_solution(966784933624377259)
XLA Ops:
  0.6 0.8 %piece.1.refs_6_ = bf16[1,144,128]{2,1,0:T(8,128)(2,1)S(1)} custom-call(bf16[128,128]{1,0:T(8,128)(2,1)} %bitcast.18, f32[1,128]{1,0:T(1,128)} %deg_hbm.1), custom_call_target="tpu_custom_call" | custom-call | tf_op jit(solution)/shard_map/piece/pallas_call | solution.py:43
  1.4 4.1 %collective-permute-start = (bf16[1,144,128]{2,1,0:T(8,128)(2,1)S(1)}, bf16[1,144,128]{2,1,0:T(8,128)(2,1)S(1)}, u32[]{:S(2)}, u32[]{:S(2)}) collective-permute-start(bf16[1,144,128]{2,1,0:T(8,128)(2,1)S(1)} %piece.1.refs_6_), channel_id=1, source_target_pairs={{0,16},{1,17},{2,18},{3,19},{4,20},{5,21},{6,22},{7,23},{8,24},{9,... | collective-permute-start | bytes 110600 | tf_op jit(solution)/shard_map/ppermute | solution.py:342
  5.5 2.7 %block_logs.3 = (f32[258,128,128]{2,1,0:T(8,128)S(1)}, s32[16]{0:T(128)S(1)}, s32[258]{0:T(512)S(1)}, f32[16,128,128]{2,1,0:T(8,128)S(1)}, s32[18]{0:T(128)S(1)}, /*index=5*/s32[160]{0:T(256)S(1)}) custom-call(bf16[4,64,128,128]{3,2,1,0:T(8,128)(2,1)} %bitcast.12, f32[16,128]{1,0:T(8,128)} %bitcast.15, s32[4,64]{1,0:T(4,128)} %bitcast.19, s32[4,64]{1,0:T(4,128)} %bitcast.22, ...), custom_call_target="tpu_custom_call" | custom-call | bytes 4194304 | tf_op jit(solution)/shard_map/block_logs/pallas_call | solution.py:169
  8.2 0.0 collective-permute-done
  8.3 1.6 %collective-permute-start.1 = (bf16[2,144,128]{2,1,0:T(8,128)(2,1)S(1)}, bf16[2,144,128]{2,1,0:T(8,128)(2,1)S(1)}, u32[]{:S(2)}, u32[]{:S(2)}) collective-permute-start(bf16[2,144,128]{2,1,0:T(8,128)(2,1)S(1)} %pad_maximum_fusion.1.refs_6_), channel_id=1, source_target_pairs={{0,8},{1,9},{2,10},{3,11},{4,12},{5,13},{6,14},{7,15},{8,0},{9,1},... | collective-permute-start | bytes 221192 | tf_op jit(solution)/shard_map/ppermute | solution.py:342
  9.9 3.7 %block_logs.4 = (f32[258,128,128]{2,1,0:T(8,128)S(1)}, s32[16]{0:T(128)S(1)}, s32[258]{0:T(512)S(1)}) custom-call(bf16[4,64,128,128]{3,2,1,0:T(8,128)(2,1)} %bitcast.13, f32[16,128]{1,0:T(8,128)} %bitcast.16, s32[4,64]{1,0:T(4,128)} %bitcast.20, s32[4,64]{1,0:T(4,128)} %bitcast.23, s32[4,64]{1,0:T(4,128)} %bitcast.26, ...), custom_call_target="tpu_custom_call", output_to_operand_aliasing={{0}: (7, {})} | custom-call | bytes 4194304 | tf_op jit(solution)/shard_map/block_logs/pallas_call | solution.py:169
  13.7 0.0 collective-permute-done.1
  13.7 1.1 %collective-permute-start.3 = (bf16[4,144,128]{2,1,0:T(8,128)(2,1)S(1)}, bf16[4,144,128]{2,1,0:T(8,128)(2,1)S(1)}, u32[]{:S(2)}, u32[]{:S(2)}) collective-permute-start(bf16[4,144,128]{2,1,0:T(8,128)(2,1)S(1)} %pad_maximum_fusion.refs_0_), channel_id=1, source_target_pairs={{0,4},{1,5},{2,6},{3,7},{4,0},{5,1},{6,2},{7,3},{8,12},{9,13},{10,... | collective-permute-start | bytes 442376 | tf_op jit(solution)/shard_map/ppermute | solution.py:342
  14.8 1.8 %collective-permute-start.2 = (bf16[4,144,128]{2,1,0:T(8,128)(2,1)S(1)}, bf16[4,144,128]{2,1,0:T(8,128)(2,1)S(1)}, u32[]{:S(2)}, u32[]{:S(2)}) collective-permute-start(bf16[4,144,128]{2,1,0:T(8,128)(2,1)S(1)} %pad_maximum_fusion.refs_0_), channel_id=1, source_target_pairs={{0,2},{1,3},{2,0},{3,1},{4,6},{5,7},{6,4},{7,5},{8,10},{9,11},{10,... | collective-permute-start | bytes 442376 | tf_op jit(solution)/shard_map/ppermute | solution.py:342
  16.5 0.0 collective-permute-start.5
  16.5 2.4 %collective-permute-done.3.refs_6_.refs_2_ = bf16[4,144,128]{2,1,0:T(8,128)(2,1)S(1)} collective-permute-done((bf16[4,144,128]{2,1,0:T(8,128)(2,1)S(1)}, bf16[4,144,128]{2,1,0:T(8,128)(2,1)S(1)}, u32[]{:S(2)}, u32[]{:S(2)}) %collective-permute-start.3) | collective-permute-done | bytes 147488 | tf_op jit(solution)/shard_map/ppermute | solution.py:342
  18.9 1.7 %collective-permute-start.4 = (bf16[4,144,128]{2,1,0:T(8,128)(2,1)S(1)}, bf16[4,144,128]{2,1,0:T(8,128)(2,1)S(1)}, u32[]{:S(2)}, u32[]{:S(2)}) collective-permute-start(bf16[4,144,128]{2,1,0:T(8,128)(2,1)S(1)} %collective-permute-done.3.refs_6_.refs_2_), channel_id=1, source_target_pairs={{0,2},{1,3},{2,0},{3,1},{4,6},{5,7},{6,4},{7,5},{8,10},{9,11},{10,... | collective-permute-start | bytes 442376 | tf_op jit(solution)/shard_map/ppermute | solution.py:342
  20.6 0.0 collective-permute-start.6
  20.6 4.0 %block_logs.5 = (f32[258,128,128]{2,1,0:T(8,128)S(1)}, s32[16]{0:T(128)}, s32[258]{0:T(512)S(1)}) custom-call(bf16[4,64,128,128]{3,2,1,0:T(8,128)(2,1)} %bitcast.14, f32[16,128]{1,0:T(8,128)} %bitcast.17, s32[4,64]{1,0:T(4,128)} %bitcast.21, s32[4,64]{1,0:T(4,128)} %bitcast.24, s32[4,64]{1,0:T(4,128)} %bitcast.27, ...), custom_call_target="tpu_custom_call", output_to_operand_aliasing={{0}: (7, {})} | custom-call | bytes 8388608 | tf_op jit(solution)/shard_map/block_logs/pallas_call | solution.py:169
  24.7 0.0 collective-permute-done.2.refs_1_
  24.7 0.0 collective-permute-done.5.refs_4_
  24.7 0.0 collective-permute-done.4.refs_3_
  24.7 0.0 collective-permute-done.6.refs_6_
  24.7 1.3 %collective-permute-start.7 = (bf16[4,144,128]{2,1,0:T(8,128)(2,1)S(1)}, bf16[4,144,128]{2,1,0:T(8,128)(2,1)S(1)}, u32[]{:S(2)}, u32[]{:S(2)}) collective-permute-start(bf16[4,144,128]{2,1,0:T(8,128)(2,1)S(1)} %collective-permute-done.2.refs_1_), channel_id=1, source_target_pairs={{0,1},{1,0},{2,3},{3,2},{4,5},{5,4},{6,7},{7,6},{8,9},{9,8},{10,11... | collective-permute-start | bytes 442376 | tf_op jit(solution)/shard_map/ppermute | solution.py:342
  26.1 0.1 collective-permute-start.8
  26.1 0.9 %collective-permute-done.7.refs_5_ = bf16[4,144,128]{2,1,0:T(8,128)(2,1)S(1)} collective-permute-done((bf16[4,144,128]{2,1,0:T(8,128)(2,1)S(1)}, bf16[4,144,128]{2,1,0:T(8,128)(2,1)S(1)}, u32[]{:S(2)}, u32[]{:S(2)}) %collective-permute-start.7) | collective-permute-done | bytes 147488 | tf_op jit(solution)/shard_map/ppermute | solution.py:342
  27.1 0.4 collective-permute-done.8.refs_7_
  27.4 3.3 %products_gram.1 = (bf16[2048,128]{1,0:T(8,128)(2,1)S(1)}, bf16[2048,128]{1,0:T(8,128)(2,1)S(1)}, f32[128,128]{1,0:T(8,128)S(1)}) custom-call(f32[258,128,128]{2,1,0:T(8,128)S(1)} %get-tuple-element.73.x_ref, s32[18]{0:T(128)S(1)} %get-tuple-element.74.off_s, s32[160]{0:T(256)S(1)} %get-tuple-element.75.item_s, s32[258]{0:T(512)S(1)} %get-tuple-element.76.tile_s, ...), custom_call_target="tpu_custom_call" | custom-call | tf_op jit(solution)/shard_map/products_gram/pallas_call | solution.py:250
  30.7 10.9 %all_to_all.10 = f32[32,4,128]{2,1,0:T(4,128)S(1)} all-to-all(f32[32,4,128]{2,1,0:T(4,128)S(1)} %bitcast.11), channel_id=1, replica_groups=mesh['rows'=8,'blk'=4] {'rows','blk'}, dimensions={0} | all-to-all | bytes 131072 | tf_op jit(solution)/shard_map/all_to_all | solution.py:348
  41.7 9.1 %all_to_all.11 = f32[32,4,128]{2,1,0:T(4,128)S(1)} all-to-all(f32[32,4,128]{2,1,0:T(4,128)S(1)} %broadcast_in_dim.4), channel_id=1, replica_groups=mesh['rows'=8,'blk'=4] {'rows','blk'}, dimensions={0} | all-to-all | bytes 131072 | tf_op jit(solution)/shard_map/all_to_all | solution.py:350
  50.8 4.9 %cholesky_basis.1 = (f32[2048,128]{1,0:T(8,128)}, f32[128,128]{1,0:T(8,128)}) custom-call(f32[128,128]{1,0:T(8,128)S(1)} %bitcast.10, bf16[2048,128]{1,0:T(8,128)(2,1)S(1)} %get-tuple-element.82.hi_ref, bf16[2048,128]{1,0:T(8,128)(2,1)S(1)} %get-tuple-element.83.lo_ref), custom_call_target="tpu_custom_call" | custom-call | tf_op jit(solution)/shard_map/cholesky_basis/pallas_call | solution.py:327
  (4 shorter events, 0.1 us)
Async XLA Ops:
  1.4 6.8 %collective-permute-start = (bf16[1,144,128]{2,1,0:T(8,128)(2,1)S(1)}, bf16[1,144,128]{2,1,0:T(8,128)(2,1)S(1)}, u32[]{:S(2)}, u32[]{:S(2)}) collective-permute-start(bf16[1,144,128]{2,1,0:T(8,128)(2,1)S(1)} %piece.1.refs_6_), channel_id=1, source_target_pairs={{0,16},{1,17},{2,18},{3,19},{4,20},{5,21},{6,22},{7,23},{8,24},{9,... | collective-permute-start | bytes 110600 | tf_op jit(solution)/shard_map/ppermute | solution.py:342
  8.3 5.4 %collective-permute-start.1 = (bf16[2,144,128]{2,1,0:T(8,128)(2,1)S(1)}, bf16[2,144,128]{2,1,0:T(8,128)(2,1)S(1)}, u32[]{:S(2)}, u32[]{:S(2)}) collective-permute-start(bf16[2,144,128]{2,1,0:T(8,128)(2,1)S(1)} %pad_maximum_fusion.1.refs_6_), channel_id=1, source_target_pairs={{0,8},{1,9},{2,10},{3,11},{4,12},{5,13},{6,14},{7,15},{8,0},{9,1},... | collective-permute-start | bytes 221192 | tf_op jit(solution)/shard_map/ppermute | solution.py:342
  13.7 5.2 %collective-permute-start.3 = (bf16[4,144,128]{2,1,0:T(8,128)(2,1)S(1)}, bf16[4,144,128]{2,1,0:T(8,128)(2,1)S(1)}, u32[]{:S(2)}, u32[]{:S(2)}) collective-permute-start(bf16[4,144,128]{2,1,0:T(8,128)(2,1)S(1)} %pad_maximum_fusion.refs_0_), channel_id=1, source_target_pairs={{0,4},{1,5},{2,6},{3,7},{4,0},{5,1},{6,2},{7,3},{8,12},{9,13},{10,... | collective-permute-start | bytes 442376 | tf_op jit(solution)/shard_map/ppermute | solution.py:342
  14.8 9.9 %collective-permute-start.2 = (bf16[4,144,128]{2,1,0:T(8,128)(2,1)S(1)}, bf16[4,144,128]{2,1,0:T(8,128)(2,1)S(1)}, u32[]{:S(2)}, u32[]{:S(2)}) collective-permute-start(bf16[4,144,128]{2,1,0:T(8,128)(2,1)S(1)} %pad_maximum_fusion.refs_0_), channel_id=1, source_target_pairs={{0,2},{1,3},{2,0},{3,1},{4,6},{5,7},{6,4},{7,5},{8,10},{9,11},{10,... | collective-permute-start | bytes 442376 | tf_op jit(solution)/shard_map/ppermute | solution.py:342
  16.5 8.2 %collective-permute-start.5 = (bf16[4,144,128]{2,1,0:T(8,128)(2,1)S(1)}, bf16[4,144,128]{2,1,0:T(8,128)(2,1)S(1)}, u32[]{:S(2)}, u32[]{:S(2)}) collective-permute-start(bf16[4,144,128]{2,1,0:T(8,128)(2,1)S(1)} %pad_maximum_fusion.refs_0_), channel_id=1, source_target_pairs={{0,1},{1,0},{2,3},{3,2},{4,5},{5,4},{6,7},{7,6},{8,9},{9,8},{10,11... | collective-permute-start | bytes 442376 | tf_op jit(solution)/shard_map/ppermute | solution.py:342
  18.9 5.8 %collective-permute-start.4 = (bf16[4,144,128]{2,1,0:T(8,128)(2,1)S(1)}, bf16[4,144,128]{2,1,0:T(8,128)(2,1)S(1)}, u32[]{:S(2)}, u32[]{:S(2)}) collective-permute-start(bf16[4,144,128]{2,1,0:T(8,128)(2,1)S(1)} %collective-permute-done.3.refs_6_.refs_2_), channel_id=1, source_target_pairs={{0,2},{1,3},{2,0},{3,1},{4,6},{5,7},{6,4},{7,5},{8,10},{9,11},{10,... | collective-permute-start | bytes 442376 | tf_op jit(solution)/shard_map/ppermute | solution.py:342
  20.6 4.1 %collective-permute-start.6 = (bf16[4,144,128]{2,1,0:T(8,128)(2,1)S(1)}, bf16[4,144,128]{2,1,0:T(8,128)(2,1)S(1)}, u32[]{:S(2)}, u32[]{:S(2)}) collective-permute-start(bf16[4,144,128]{2,1,0:T(8,128)(2,1)S(1)} %collective-permute-done.3.refs_6_.refs_2_), channel_id=1, source_target_pairs={{0,1},{1,0},{2,3},{3,2},{4,5},{5,4},{6,7},{7,6},{8,9},{9,8},{10,11... | collective-permute-start | bytes 442376 | tf_op jit(solution)/shard_map/ppermute | solution.py:342
  24.7 2.3 %collective-permute-start.7 = (bf16[4,144,128]{2,1,0:T(8,128)(2,1)S(1)}, bf16[4,144,128]{2,1,0:T(8,128)(2,1)S(1)}, u32[]{:S(2)}, u32[]{:S(2)}) collective-permute-start(bf16[4,144,128]{2,1,0:T(8,128)(2,1)S(1)} %collective-permute-done.2.refs_1_), channel_id=1, source_target_pairs={{0,1},{1,0},{2,3},{3,2},{4,5},{5,4},{6,7},{7,6},{8,9},{9,8},{10,11... | collective-permute-start | bytes 442376 | tf_op jit(solution)/shard_map/ppermute | solution.py:342
  26.1 1.4 %collective-permute-start.8 = (bf16[4,144,128]{2,1,0:T(8,128)(2,1)S(1)}, bf16[4,144,128]{2,1,0:T(8,128)(2,1)S(1)}, u32[]{:S(2)}, u32[]{:S(2)}) collective-permute-start(bf16[4,144,128]{2,1,0:T(8,128)(2,1)S(1)} %collective-permute-done.4.refs_3_), channel_id=1, source_target_pairs={{0,1},{1,0},{2,3},{3,2},{4,5},{5,4},{6,7},{7,6},{8,9},{9,8},{10,11... | collective-permute-start | bytes 442376 | tf_op jit(solution)/shard_map/ppermute | solution.py:342

commit v5 on v4

--- a/solution.py
+++ b/solution.py
@@ -335,7 +335,7 @@
 
 
 AXES = ("rows", "blk")
-STAGES = ((0, 1), (1, 2), (0, 0), (2, 4))
+STAGES = ((0, 2), (2, 3), (0, 0), (3, 4))
 
 
 def send(x, mask, n_dev):

time: 56.1 us -> 55.6 us (level)
  Pallas kernels: 19.5 us -> 20.8 us
  starting transfers between devices: 11.7 us -> 10.8 us
    ppermute x9, starting transfers between devices: 11.7 us -> 10.8 us  [send(): return lax.ppermute(x, AXES, [(i, i ^ mask) for i in range(n_dev)])]
    pallas_call x3, Pallas kernels: 10.5 us -> 11.3 us  [block_logs(): pl.pallas_call(functools.partial(logs_kernel, slabs, first, place), out_s...]
  transfers between devices with their start and end apart: 9 -> 9, of which waited for: 3 -> 4; matrix products, arithmetic and copies ran while one was open for 0% -> 0% of each run, Pallas kernels for 19% -> 20%
where the time goes in v5:
time: 55.6 us; the launch traced here: 55.4 us
  Pallas kernels  20.8 us (37%)
  blocking collectives  19.8 us (36%)
  starting transfers between devices  10.8 us (19%)
  waiting for transfers between devices  3.13 us (6%)
  between operations  0.72 us (1%)
    pallas_call x3, Pallas kernels, block_logs(): pl.pallas_call(functools.partial(logs_kernel, slabs, first, place), out_s...  11.3 us
    ppermute x9, starting transfers between devices, send(): return lax.ppermute(x, AXES, [(i, i ^ mask) for i in range(n_dev)])  10.8 us
    all_to_all x1, blocking collectives, sum_all(): mine = lax.all_to_all(shares, AXES, 0, 0, tiled=True).sum(axis=0)  10.7 us
    all_to_all x1, blocking collectives, sum_all(): return lax.all_to_all(sent, AXES, 0, 0, tiled=True).reshape(x.shape)  9.1 us
    pallas_call x1, Pallas kernels, solve(): pl.pallas_call(functools.partial(solve_kernel, nb, root, chunk), out_shap...  4.94 us
    pallas_call x1, Pallas kernels, products(): pl.pallas_call(products_kernel, out_shape=(jax.ShapeDtypeStruct((bands *...  3.83 us
    ppermute x9, waiting for transfers between devices, send(): return lax.ppermute(x, AXES, [(i, i ^ mask) for i in range(n_dev)])  3.13 us
  transfers between devices with their start and end apart: 9, of which 4 were waited for; matrix products, arithmetic and copies ran while one was open for 0% of the time, Pallas kernels for 20%

profile of v5, /device:TPU:0, one launch (start us, length us, event | category | flops | bytes accessed | tf_op | source)
XLA Modules:
  0.0 55.4 jit_solution(8228692817007838366)
XLA Ops:
  0.6 0.8 %piece.1.refs_6_ = bf16[1,144,128]{2,1,0:T(8,128)(2,1)S(1)} custom-call(bf16[128,128]{1,0:T(8,128)(2,1)} %bitcast.18, f32[1,128]{1,0:T(1,128)} %deg_hbm.1), custom_call_target="tpu_custom_call" | custom-call | tf_op jit(solution)/shard_map/piece/pallas_call | solution.py:43
  1.4 4.1 %collective-permute-start = (bf16[1,144,128]{2,1,0:T(8,128)(2,1)S(1)}, bf16[1,144,128]{2,1,0:T(8,128)(2,1)S(1)}, u32[]{:S(2)}, u32[]{:S(2)}) collective-permute-start(bf16[1,144,128]{2,1,0:T(8,128)(2,1)S(1)} %piece.1.refs_6_), channel_id=1, source_target_pairs={{0,16},{1,17},{2,18},{3,19},{4,20},{5,21},{6,22},{7,23},{8,24},{9,... | collective-permute-start | bytes 110600 | tf_op jit(solution)/shard_map/ppermute | solution.py:342
  5.5 4.3 %block_logs.3 = (f32[258,128,128]{2,1,0:T(8,128)S(1)}, s32[16]{0:T(128)S(1)}, s32[258]{0:T(512)S(1)}, f32[16,128,128]{2,1,0:T(8,128)S(1)}, s32[18]{0:T(128)S(1)}, /*index=5*/s32[160]{0:T(256)S(1)}) custom-call(bf16[4,64,128,128]{3,2,1,0:T(8,128)(2,1)} %bitcast.12, f32[16,128]{1,0:T(8,128)} %bitcast.15, s32[4,64]{1,0:T(4,128)} %bitcast.19, s32[4,64]{1,0:T(4,128)} %bitcast.22, ...), custom_call_target="tpu_custom_call" | custom-call | bytes 8388608 | tf_op jit(solution)/shard_map/block_logs/pallas_call | solution.py:169
  9.8 0.0 collective-permute-done
  9.8 1.2 %collective-permute-start.1 = (bf16[2,144,128]{2,1,0:T(8,128)(2,1)S(1)}, bf16[2,144,128]{2,1,0:T(8,128)(2,1)S(1)}, u32[]{:S(2)}, u32[]{:S(2)}) collective-permute-start(bf16[2,144,128]{2,1,0:T(8,128)(2,1)S(1)} %pad_maximum_fusion.1.refs_6_), channel_id=1, source_target_pairs={{0,8},{1,9},{2,10},{3,11},{4,12},{5,13},{6,14},{7,15},{8,0},{9,1},... | collective-permute-start | bytes 221192 | tf_op jit(solution)/shard_map/ppermute | solution.py:342
  11.0 3.7 %block_logs.4 = (f32[258,128,128]{2,1,0:T(8,128)S(1)}, s32[16]{0:T(128)S(1)}, s32[258]{0:T(512)S(1)}) custom-call(bf16[4,64,128,128]{3,2,1,0:T(8,128)(2,1)} %bitcast.13, f32[16,128]{1,0:T(8,128)} %bitcast.16, s32[4,64]{1,0:T(4,128)} %bitcast.20, s32[4,64]{1,0:T(4,128)} %bitcast.23, s32[4,64]{1,0:T(4,128)} %bitcast.26, ...), custom_call_target="tpu_custom_call", output_to_operand_aliasing={{0}: (7, {})} | custom-call | bytes 4194304 | tf_op jit(solution)/shard_map/block_logs/pallas_call | solution.py:169
  14.7 0.0 collective-permute-done.1
  14.8 0.8 %collective-permute-start.3 = (bf16[4,144,128]{2,1,0:T(8,128)(2,1)S(1)}, bf16[4,144,128]{2,1,0:T(8,128)(2,1)S(1)}, u32[]{:S(2)}, u32[]{:S(2)}) collective-permute-start(bf16[4,144,128]{2,1,0:T(8,128)(2,1)S(1)} %pad_maximum_fusion.refs_0_), channel_id=1, source_target_pairs={{0,4},{1,5},{2,6},{3,7},{4,0},{5,1},{6,2},{7,3},{8,12},{9,13},{10,... | collective-permute-start | bytes 442376 | tf_op jit(solution)/shard_map/ppermute | solution.py:342
  15.6 2.7 %collective-permute-start.2 = (bf16[4,144,128]{2,1,0:T(8,128)(2,1)S(1)}, bf16[4,144,128]{2,1,0:T(8,128)(2,1)S(1)}, u32[]{:S(2)}, u32[]{:S(2)}) collective-permute-start(bf16[4,144,128]{2,1,0:T(8,128)(2,1)S(1)} %pad_maximum_fusion.refs_0_), channel_id=1, source_target_pairs={{0,2},{1,3},{2,0},{3,1},{4,6},{5,7},{6,4},{7,5},{8,10},{9,11},{10,... | collective-permute-start | bytes 442376 | tf_op jit(solution)/shard_map/ppermute | solution.py:342
  18.3 0.0 collective-permute-start.5
  18.3 1.7 %collective-permute-done.3.refs_6_.refs_2_ = bf16[4,144,128]{2,1,0:T(8,128)(2,1)S(1)} collective-permute-done((bf16[4,144,128]{2,1,0:T(8,128)(2,1)S(1)}, bf16[4,144,128]{2,1,0:T(8,128)(2,1)S(1)}, u32[]{:S(2)}, u32[]{:S(2)}) %collective-permute-start.3) | collective-permute-done | bytes 147488 | tf_op jit(solution)/shard_map/ppermute | solution.py:342
  20.0 1.5 %collective-permute-start.4 = (bf16[4,144,128]{2,1,0:T(8,128)(2,1)S(1)}, bf16[4,144,128]{2,1,0:T(8,128)(2,1)S(1)}, u32[]{:S(2)}, u32[]{:S(2)}) collective-permute-start(bf16[4,144,128]{2,1,0:T(8,128)(2,1)S(1)} %collective-permute-done.3.refs_6_.refs_2_), channel_id=1, source_target_pairs={{0,2},{1,3},{2,0},{3,1},{4,6},{5,7},{6,4},{7,5},{8,10},{9,11},{10,... | collective-permute-start | bytes 442376 | tf_op jit(solution)/shard_map/ppermute | solution.py:342
  21.4 0.0 collective-permute-start.6
  21.4 3.2 %block_logs.5 = (f32[258,128,128]{2,1,0:T(8,128)S(1)}, s32[16]{0:T(128)}, s32[258]{0:T(512)S(1)}) custom-call(bf16[4,64,128,128]{3,2,1,0:T(8,128)(2,1)} %bitcast.14, f32[16,128]{1,0:T(8,128)} %bitcast.17, s32[4,64]{1,0:T(4,128)} %bitcast.21, s32[4,64]{1,0:T(4,128)} %bitcast.24, s32[4,64]{1,0:T(4,128)} %bitcast.27, ...), custom_call_target="tpu_custom_call", output_to_operand_aliasing={{0}: (7, {})} | custom-call | bytes 4194304 | tf_op jit(solution)/shard_map/block_logs/pallas_call | solution.py:169
  24.7 0.0 collective-permute-done.2.refs_1_
  24.7 0.0 collective-permute-done.5.refs_4_
  24.7 0.4 collective-permute-done.4.refs_3_
  25.1 0.0 collective-permute-done.6.refs_6_
  25.1 0.2 collective-permute-start.7
  25.3 0.3 collective-permute-start.8
  25.6 0.9 %collective-permute-done.7.refs_5_ = bf16[4,144,128]{2,1,0:T(8,128)(2,1)S(1)} collective-permute-done((bf16[4,144,128]{2,1,0:T(8,128)(2,1)S(1)}, bf16[4,144,128]{2,1,0:T(8,128)(2,1)S(1)}, u32[]{:S(2)}, u32[]{:S(2)}) %collective-permute-start.7) | collective-permute-done | bytes 147488 | tf_op jit(solution)/shard_map/ppermute | solution.py:342
  26.5 0.2 collective-permute-done.8.refs_7_
  26.7 3.8 %products_gram.1 = (bf16[2048,128]{1,0:T(8,128)(2,1)S(1)}, bf16[2048,128]{1,0:T(8,128)(2,1)S(1)}, f32[128,128]{1,0:T(8,128)S(1)}) custom-call(f32[258,128,128]{2,1,0:T(8,128)S(1)} %get-tuple-element.73.x_ref, s32[18]{0:T(128)S(1)} %get-tuple-element.74.off_s, s32[160]{0:T(256)S(1)} %get-tuple-element.75.item_s, s32[258]{0:T(512)S(1)} %get-tuple-element.76.tile_s, ...), custom_call_target="tpu_custom_call" | custom-call | tf_op jit(solution)/shard_map/products_gram/pallas_call | solution.py:250
  30.5 10.7 %all_to_all.10 = f32[32,4,128]{2,1,0:T(4,128)S(1)} all-to-all(f32[32,4,128]{2,1,0:T(4,128)S(1)} %bitcast.11), channel_id=1, replica_groups=mesh['rows'=8,'blk'=4] {'rows','blk'}, dimensions={0} | all-to-all | bytes 131072 | tf_op jit(solution)/shard_map/all_to_all | solution.py:348
  41.3 9.1 %all_to_all.11 = f32[32,4,128]{2,1,0:T(4,128)S(1)} all-to-all(f32[32,4,128]{2,1,0:T(4,128)S(1)} %broadcast_in_dim.4), channel_id=1, replica_groups=mesh['rows'=8,'blk'=4] {'rows','blk'}, dimensions={0} | all-to-all | bytes 131072 | tf_op jit(solution)/shard_map/all_to_all | solution.py:350
  50.4 4.9 %cholesky_basis.1 = (f32[2048,128]{1,0:T(8,128)}, f32[128,128]{1,0:T(8,128)}) custom-call(f32[128,128]{1,0:T(8,128)S(1)} %bitcast.10, bf16[2048,128]{1,0:T(8,128)(2,1)S(1)} %get-tuple-element.82.hi_ref, bf16[2048,128]{1,0:T(8,128)(2,1)S(1)} %get-tuple-element.83.lo_ref), custom_call_target="tpu_custom_call" | custom-call | tf_op jit(solution)/shard_map/cholesky_basis/pallas_call | solution.py:327
  (4 shorter events, 0.1 us)
Async XLA Ops:
  1.4 8.4 %collective-permute-start = (bf16[1,144,128]{2,1,0:T(8,128)(2,1)S(1)}, bf16[1,144,128]{2,1,0:T(8,128)(2,1)S(1)}, u32[]{:S(2)}, u32[]{:S(2)}) collective-permute-start(bf16[1,144,128]{2,1,0:T(8,128)(2,1)S(1)} %piece.1.refs_6_), channel_id=1, source_target_pairs={{0,16},{1,17},{2,18},{3,19},{4,20},{5,21},{6,22},{7,23},{8,24},{9,... | collective-permute-start | bytes 110600 | tf_op jit(solution)/shard_map/ppermute | solution.py:342
  9.8 4.9 %collective-permute-start.1 = (bf16[2,144,128]{2,1,0:T(8,128)(2,1)S(1)}, bf16[2,144,128]{2,1,0:T(8,128)(2,1)S(1)}, u32[]{:S(2)}, u32[]{:S(2)}) collective-permute-start(bf16[2,144,128]{2,1,0:T(8,128)(2,1)S(1)} %pad_maximum_fusion.1.refs_6_), channel_id=1, source_target_pairs={{0,8},{1,9},{2,10},{3,11},{4,12},{5,13},{6,14},{7,15},{8,0},{9,1},... | collective-permute-start | bytes 221192 | tf_op jit(solution)/shard_map/ppermute | solution.py:342
  14.8 5.2 %collective-permute-start.3 = (bf16[4,144,128]{2,1,0:T(8,128)(2,1)S(1)}, bf16[4,144,128]{2,1,0:T(8,128)(2,1)S(1)}, u32[]{:S(2)}, u32[]{:S(2)}) collective-permute-start(bf16[4,144,128]{2,1,0:T(8,128)(2,1)S(1)} %pad_maximum_fusion.refs_0_), channel_id=1, source_target_pairs={{0,4},{1,5},{2,6},{3,7},{4,0},{5,1},{6,2},{7,3},{8,12},{9,13},{10,... | collective-permute-start | bytes 442376 | tf_op jit(solution)/shard_map/ppermute | solution.py:342
  15.6 9.1 %collective-permute-start.2 = (bf16[4,144,128]{2,1,0:T(8,128)(2,1)S(1)}, bf16[4,144,128]{2,1,0:T(8,128)(2,1)S(1)}, u32[]{:S(2)}, u32[]{:S(2)}) collective-permute-start(bf16[4,144,128]{2,1,0:T(8,128)(2,1)S(1)} %pad_maximum_fusion.refs_0_), channel_id=1, source_target_pairs={{0,2},{1,3},{2,0},{3,1},{4,6},{5,7},{6,4},{7,5},{8,10},{9,11},{10,... | collective-permute-start | bytes 442376 | tf_op jit(solution)/shard_map/ppermute | solution.py:342
  18.3 6.4 %collective-permute-start.5 = (bf16[4,144,128]{2,1,0:T(8,128)(2,1)S(1)}, bf16[4,144,128]{2,1,0:T(8,128)(2,1)S(1)}, u32[]{:S(2)}, u32[]{:S(2)}) collective-permute-start(bf16[4,144,128]{2,1,0:T(8,128)(2,1)S(1)} %pad_maximum_fusion.refs_0_), channel_id=1, source_target_pairs={{0,1},{1,0},{2,3},{3,2},{4,5},{5,4},{6,7},{7,6},{8,9},{9,8},{10,11... | collective-permute-start | bytes 442376 | tf_op jit(solution)/shard_map/ppermute | solution.py:342
  20.0 5.1 %collective-permute-start.4 = (bf16[4,144,128]{2,1,0:T(8,128)(2,1)S(1)}, bf16[4,144,128]{2,1,0:T(8,128)(2,1)S(1)}, u32[]{:S(2)}, u32[]{:S(2)}) collective-permute-start(bf16[4,144,128]{2,1,0:T(8,128)(2,1)S(1)} %collective-permute-done.3.refs_6_.refs_2_), channel_id=1, source_target_pairs={{0,2},{1,3},{2,0},{3,1},{4,6},{5,7},{6,4},{7,5},{8,10},{9,11},{10,... | collective-permute-start | bytes 442376 | tf_op jit(solution)/shard_map/ppermute | solution.py:342
  21.4 3.7 %collective-permute-start.6 = (bf16[4,144,128]{2,1,0:T(8,128)(2,1)S(1)}, bf16[4,144,128]{2,1,0:T(8,128)(2,1)S(1)}, u32[]{:S(2)}, u32[]{:S(2)}) collective-permute-start(bf16[4,144,128]{2,1,0:T(8,128)(2,1)S(1)} %collective-permute-done.3.refs_6_.refs_2_), channel_id=1, source_target_pairs={{0,1},{1,0},{2,3},{3,2},{4,5},{5,4},{6,7},{7,6},{8,9},{9,8},{10,11... | collective-permute-start | bytes 442376 | tf_op jit(solution)/shard_map/ppermute | solution.py:342
  25.1 1.4 %collective-permute-start.7 = (bf16[4,144,128]{2,1,0:T(8,128)(2,1)S(1)}, bf16[4,144,128]{2,1,0:T(8,128)(2,1)S(1)}, u32[]{:S(2)}, u32[]{:S(2)}) collective-permute-start(bf16[4,144,128]{2,1,0:T(8,128)(2,1)S(1)} %collective-permute-done.2.refs_1_), channel_id=1, source_target_pairs={{0,1},{1,0},{2,3},{3,2},{4,5},{5,4},{6,7},{7,6},{8,9},{9,8},{10,11... | collective-permute-start | bytes 442376 | tf_op jit(solution)/shard_map/ppermute | solution.py:342
  25.3 1.4 %collective-permute-start.8 = (bf16[4,144,128]{2,1,0:T(8,128)(2,1)S(1)}, bf16[4,144,128]{2,1,0:T(8,128)(2,1)S(1)}, u32[]{:S(2)}, u32[]{:S(2)}) collective-permute-start(bf16[4,144,128]{2,1,0:T(8,128)(2,1)S(1)} %collective-permute-done.4.refs_3_), channel_id=1, source_target_pairs={{0,1},{1,0},{2,3},{3,2},{4,5},{5,4},{6,7},{7,6},{8,9},{9,8},{10,11... | collective-permute-start | bytes 442376 | tf_op jit(solution)/shard_map/ppermute | solution.py:342
